TPU v7x, 128 devices: a whole 4x4x4 slice. The times are simulated.
128 devices in a mesh: node: 8 (over x, core), local: 16 (over z, y).
Axes of the slice: x: 4, y: 4, z: 4, core: 2. Of those that a mesh axis runs over, the one named last changes fastest.
Arguments:
- tokens: bfloat16 [2048, 3584], P(('node', 'local')), may hold values from -6 to 6
- route: int32 [2048, 8], P(('node', 'local')), may hold values from 0 to 127, as said below
- combine_weight: bfloat16 [2048, 8], P(('node', 'local')), may hold values from 0.049804688 to 0.5
- gate_up: bfloat16 [128, 3584, 2048], P(('node', 'local')), may hold values from -0.09375 to 0.09375
- down: bfloat16 [128, 1024, 3584], P(('node', 'local')), may hold values from -0.1875 to 0.1875
Outputs:
- mixed: bfloat16 [2048, 3584], P(('node', 'local'))
Inputs may be any that keep to these rules, and one draw needn't show every extreme that they name: `route`: expert e is held by device e in node-major order, so it lies on node e // 16. Each row names 8 different experts on exactly four nodes, two on each node. Among the rows of one device no expert is named more than 2 times; among the rows of the 8 devices that share one local index no expert is named more than 16 times; both bounds are reached in every draw.
All inputs are finite; a program needn't handle non-finite values.
Results may differ from a plain program's by a relative error of at most 0.012.
Values may be sent and summed in bfloat16 or wider, within the bound.
No kernel may reach another device: no remote copies, remote signals or barrier semaphores. Data moves between devices by JAX's collectives and lax.ppermute only.
A program may use at most 64 MiB of HBM per device.

v0:
```python
import jax
import jax.numpy as jnp
from jax import lax
from jax.sharding import PartitionSpec as P


def expert_rows(rows, gate_up, down):
    hidden_count = down.shape[0]
    hidden = jnp.dot(rows, gate_up, preferred_element_type=jnp.float32)
    active = (jax.nn.silu(hidden[:, :hidden_count]) * hidden[:, hidden_count:]).astype(jnp.bfloat16)
    return jnp.dot(active, down, preferred_element_type=jnp.float32).astype(jnp.bfloat16)


def node_combine(outputs, route, combine_weight, node_count, per_node):
    node_pick = route // per_node
    member = (
        node_pick[:, :, None] == jnp.arange(node_count, dtype=jnp.int32)[None, None, :]
    ).astype(jnp.float32)
    coefficient = member * combine_weight.astype(jnp.float32)[:, :, None]
    partial_value = jnp.einsum("rkm,rkd->rmd", coefficient, outputs.astype(jnp.float32)).astype(
        jnp.bfloat16
    )
    return jnp.sum(partial_value.astype(jnp.float32), axis=1).astype(jnp.bfloat16)


def slot_rank(hit_flags):
    return jnp.cumsum(hit_flags, axis=0) - hit_flags


def on_device(tokens, route, combine_weight, gate_up, down):
    row_count, model_width = tokens.shape
    top_count = route.shape[1]
    node_count = lax.axis_size("node")
    local_count = lax.axis_size("local")
    own_gate_up = gate_up[0]
    own_down = down[0]
    peer_count = node_count * local_count
    capacity = 16 * row_count // peer_count
    flat_route = route.reshape(-1)
    hit_flags = (flat_route[:, None] == jnp.arange(peer_count, dtype=jnp.int32)[None, :]).astype(
        jnp.int32
    )
    ranks = jnp.sum(slot_rank(hit_flags) * hit_flags, axis=1)
    source = jnp.arange(row_count * top_count, dtype=jnp.int32) // top_count
    slot_ids = jnp.arange(peer_count * capacity, dtype=jnp.int32)
    matches = (
        (flat_route[:, None] == (slot_ids // capacity)[None, :])
        & (ranks[:, None] == (slot_ids % capacity)[None, :])
    ).astype(jnp.int32)
    fill_source = jnp.sum(matches * source[:, None], axis=0)
    slot_live = jnp.sum(matches, axis=0) > 0
    send_rows = jnp.where(
        slot_live[:, None], tokens[fill_source], jnp.zeros((), jnp.bfloat16)
    ).reshape(peer_count, capacity, model_width)
    got_rows = lax.all_to_all(send_rows, ("node", "local"), split_axis=0, concat_axis=0, tiled=True)
    lead_shape = got_rows.shape[:2]
    flat_rows = got_rows.reshape(-1, model_width)
    results = expert_rows(flat_rows, own_gate_up, own_down)
    results = results.reshape(lead_shape + (model_width,))
    returned = lax.all_to_all(results, ("node", "local"), split_axis=0, concat_axis=0, tiled=True)
    outputs = returned[flat_route, ranks].reshape(row_count, top_count, model_width)
    return node_combine(outputs, route, combine_weight, node_count, local_count)


def solution(mesh):
    in_specs = (
        P(("node", "local"), None),
        P(("node", "local"), None),
        P(("node", "local"), None),
        P(("node", "local"), None, None),
        P(("node", "local"), None, None),
    )
    out_specs = P(("node", "local"), None)
    return jax.shard_map(
        on_device, mesh=mesh, in_specs=in_specs, out_specs=out_specs, check_vma=False
    )
```

profile of v0, /device:TPU:0, one launch (start us, length us, event | category | flops | bytes accessed | tf_op | source)
XLA Modules:
  0.0 98.2 jit_solution(6409717340241719393)
XLA Ops:
  0.0 0.0 copy-start
  0.0 0.8 copy.16
  0.8 0.1 eq.59
  0.9 0.1 fusion.12
  1.0 0.2 reduce_window_sum.11
  1.2 0.2 select_reduce_fusion.1
  1.3 0.1 convert_reduce_fusion
  1.5 0.0 copy-done
  1.5 1.7 %gather_fusion = bf16[256,3584]{1,0:T(8,128)(2,1)S(1)} fusion(bf16[16,3584]{1,0:T(8,128)(2,1)S(1)} %copy-done, s32[1024]{0:T(1024)S(1)} %pad_clamp_fusion), kind=kCustom, calls=%fused_computation | custom fusion | bytes 3671040 | tf_op jit(solution)/shard_map/gather | solution.py:53
  3.2 1.7 %gather.9 = bf16[128,2,3584]{2,1,0:T(2,128)(2,1)} reshape(bf16[256,3584]{1,0:T(8,128)(2,1)S(1)} %gather_fusion) | data formatting | bytes 3670016 | tf_op jit(solution)/shard_map/gather | solution.py:53
  4.9 0.2 gt.11
  5.1 3.3 %broadcast_select_fusion = bf16[128,2,3584]{2,1,0:T(2,128)(2,1)S(1)} fusion(bf16[128,2,3584]{2,1,0:T(2,128)(2,1)} %gather.9, pred[128,2]{1,0:T(8,128)(4,1)S(1)} %gt.11), kind=kLoop, calls=%fused_computation.8 | loop fusion | flops 917504 | bytes 3670272 | tf_op jit(solution)/shard_map/jit(_where)/select_n | solution.py:52
  8.4 38.0 %all_to_all.10 = bf16[128,2,3584]{2,1,0:T(2,128)(2,1)S(1)} all-to-all(bf16[128,2,3584]{2,1,0:T(2,128)(2,1)S(1)} %broadcast_select_fusion), channel_id=1, replica_groups=mesh['node'=8,'local'=16] {'node','local'}, dimensions={0} | all-to-all | bytes 3670016 | tf_op jit(solution)/shard_map/all_to_all | solution.py:55
  46.4 1.7 %reshape.118 = bf16[256,3584]{1,0:T(8,128)(2,1)} reshape(bf16[128,2,3584]{2,1,0:T(2,128)(2,1)S(1)} %all_to_all.10) | data formatting | bytes 3670016 | tf_op jit(solution)/shard_map/reshape | solution.py:57
  48.1 7.8 %fusion = f32[256,2048]{1,0:T(8,128)S(1)} fusion(bf16[256,3584]{1,0:T(8,128)(2,1)} %reshape.118, bf16[1,3584,2048]{2,1,0:T(8,128)(2,1)} %param.8), kind=kOutput, calls=%fused_computation.2 | convolution fusion | flops 3758096384 | bytes 18612224 | tf_op jit(solution)/shard_map/dot_general | solution.py:9
  55.8 5.2 %fusion.4 = bf16[256,3584]{1,0:T(8,128)(2,1)S(1)} fusion(bf16[1,1024,3584]{2,1,0:T(8,128)(2,1)} %param.9, f32[256,2048]{1,0:T(8,128)S(1)} %fusion), kind=kOutput, calls=%fused_computation.6 | convolution fusion | flops 1881538560 | bytes 11272192 | tf_op jit(solution)/shard_map/dot_general | solution.py:11
  61.1 1.7 %reshape.119 = bf16[128,2,3584]{2,1,0:T(2,128)(2,1)} reshape(bf16[256,3584]{1,0:T(8,128)(2,1)S(1)} %fusion.4) | data formatting | bytes 3670016 | tf_op jit(solution)/shard_map/reshape | solution.py:59
  62.8 0.0 copy-start.1
  62.8 0.0 copy-start.2
  62.8 4.8 %all-to-all-start.1 = ((bf16[128,2,3584]{2,1,0:T(2,128)(2,1)}), bf16[128,2,3584]{2,1,0:T(2,128)(2,1)S(1)}, u32[]{:S(2)}, u32[]{:S(2)}) async-start(bf16[128,2,3584]{2,1,0:T(2,128)(2,1)} %reshape.119), calls=%async_computation.1 | async-start | bytes 3670016 | tf_op jit(solution)/shard_map/all_to_all | solution.py:60
  67.5 0.1 reshape.120
  67.6 0.0 copy-done.1
  67.7 0.1 copy.14
  67.7 0.0 copy-done.2
  67.7 0.1 copy.15
  67.8 26.8 %all-to-all-done.1 = bf16[128,2,3584]{2,1,0:T(2,128)(2,1)S(1)} async-done(((bf16[128,2,3584]{2,1,0:T(2,128)(2,1)}), bf16[128,2,3584]{2,1,0:T(2,128)(2,1)S(1)}, u32[]{:S(2)}, u32[]{:S(2)}) %all-to-all-start.1) | async-done | bytes 1835040 | tf_op jit(solution)/shard_map/all_to_all | solution.py:60
  94.6 2.3 %gather_fusion.1 = bf16[128,3584]{1,0:T(8,128)(2,1)S(1)} fusion(bf16[128,2,3584]{2,1,0:T(2,128)(2,1)S(1)} %all-to-all-done.1, s32[128]{0:T(128)S(1)} %fusion.26), kind=kCustom, calls=%fused_computation.1 | custom fusion | bytes 1836032 | tf_op jit(solution)/shard_map/gather | solution.py:61
  97.0 1.3 %fusion.7 = bf16[16,3584]{1,0:T(8,128)(2,1)} fusion(bf16[128,3584]{1,0:T(8,128)(2,1)S(1)} %gather_fusion.1, bf16[16,8]{1,0:T(8,128)(2,1)S(1)} %copy.15, s32[16,8]{1,0:T(8,128)S(1)} %copy.14), kind=kOutput, calls=%fused_computation.9 | convolution fusion | flops 7743488 | bytes 1032960 | tf_op jit(solution)/shard_map/rkm,rkd->rmd/dot_general | solution.py:20
  (7 shorter events, 0.0 us)
Async XLA Ops:
  0.0 1.5 %copy-start = (bf16[16,3584]{1,0:T(8,128)(2,1)S(1)}, bf16[16,3584]{1,0:T(8,128)(2,1)}, u32[]{:S(2)}) copy-start(bf16[16,3584]{1,0:T(8,128)(2,1)} %param.5) | copy-start | bytes 344068
  62.8 4.9 %copy-start.1 = (s32[16,8]{0,1:T(8,128)S(1)}, s32[16,8]{0,1:T(8,128)}, u32[]{:S(2)}) copy-start(s32[16,8]{0,1:T(8,128)} %param.6) | copy-start | bytes 1540
  62.8 5.0 %copy-start.2 = (bf16[16,8]{0,1:T(8,128)(2,1)S(1)}, bf16[16,8]{0,1:T(8,128)(2,1)}, u32[]{:S(2)}) copy-start(bf16[16,8]{0,1:T(8,128)(2,1)} %param.7) | copy-start | bytes 772
  62.8 31.9 %all-to-all-start.1 = ((bf16[128,2,3584]{2,1,0:T(2,128)(2,1)}), bf16[128,2,3584]{2,1,0:T(2,128)(2,1)S(1)}, u32[]{:S(2)}, u32[]{:S(2)}) async-start(bf16[128,2,3584]{2,1,0:T(2,128)(2,1)} %reshape.119), calls=%async_computation.1 | async-start | bytes 3670016 | tf_op jit(solution)/shard_map/all_to_all | solution.py:60
where the time goes:
time: 98.5 us; the launch traced here: 98.2 us
  blocking collectives  38 us (39%)
  waiting for transfers between devices  26.8 us (27%)
  matrix products  14.3 us (15%)
  local copies, waits for them, and re-layouts  10.4 us (11%)
  starting transfers between devices  4.78 us (5%)
  other arithmetic  3.87 us (4%)
    all_to_all x1, blocking collectives, on_device(): lax.all_to_all(send_rows, ('node', 'local'), split_axis=0, concat_axis=0,...  38 us
    all_to_all x1, waiting for transfers between devices, on_device(): lax.all_to_all(results, ('node', 'local'), split_axis=0, concat_axis=0, t...  26.8 us
    dot_general x1, matrix products, expert_rows(): hidden = jnp.dot(rows, gate_up, preferred_element_type=jnp.float32)  7.77 us
    dot_general x1, matrix products, expert_rows(): jnp.dot(active, down, preferred_element_type=jnp.float32)  5.22 us
    all_to_all x1, starting transfers between devices, on_device(): lax.all_to_all(results, ('node', 'local'), split_axis=0, concat_axis=0, t...  4.78 us
    gather x2, local copies, waits for them, and re-layouts, on_device(): tokens[fill_source]  3.4 us
    select_n x1, other arithmetic, on_device(): jnp.where(slot_live[:, None], tokens[fill_source], jnp.zeros((), jnp.bflo...  3.26 us
    gather x1, local copies, waits for them, and re-layouts, on_device(): returned[flat_route, ranks].reshape(row_count, top_count, model_width)  2.33 us
  transfers between devices with their start and end apart: 1, of which 1 were waited for; matrix products, arithmetic and copies ran while one was open for 0% of the time, Pallas kernels for 0%

commit v1 on v0

v1 whole, which is shorter than its diff:
```python
import functools

import jax
import jax.numpy as jnp
from jax import lax
from jax.experimental import pallas as pl
from jax.experimental.pallas import tpu as pltpu
from jax.sharding import PartitionSpec as P

LANES = 128
F32 = jnp.float32
BF16 = jnp.bfloat16


def pack_kernel(route_ref, tokens_ref, out_ref, rank_ref, low, high, source):
    top_count, row_count = route_ref.shape
    chunks = tokens_ref.shape[1] // LANES
    pitch = 2 * chunks
    peers = out_ref.shape[0] // pitch

    low[...] = jnp.zeros_like(low)
    high[...] = jnp.zeros_like(high)
    for c in range(chunks):
        part = tokens_ref[:, c * LANES : (c + 1) * LANES].astype(F32)
        low[pl.ds(2 * c, row_count, stride=pitch), :] = part
        high[pl.ds(2 * c + 1, row_count, stride=pitch), :] = part

    def clear(i, _):
        source[i] = row_count
        return 0

    lax.fori_loop(0, 2 * peers, clear, 0, unroll=16)

    def place(t, _):
        for k in range(top_count):
            e = route_ref[k, t]
            r = jnp.where(source[e] == row_count, 0, 1)
            source[r * peers + e] = t
            rank_ref[k, t] = r
        return 0

    lax.fori_loop(0, row_count, place, 0)

    def fill(i, _):
        blocks = []
        for p in (2 * i, 2 * i + 1):
            a = pl.multiple_of(source[p] * pitch, 8)
            b = pl.multiple_of(source[peers + p] * pitch, 8)
            blocks.append(low[pl.ds(a, pitch), :] + high[pl.ds(b, pitch), :])
        out_ref[pl.ds(pl.multiple_of(i * 2 * pitch, 16), 2 * pitch), :] = jnp.concatenate(
            blocks, axis=0
        ).astype(BF16)
        return 0

    lax.fori_loop(0, peers // 2, fill, 0, unroll=2)


def pack(route, tokens, peers):
    row_count, width = tokens.shape
    pitch = 2 * width // LANES
    return pl.pallas_call(
        pack_kernel,
        out_shape=(
            jax.ShapeDtypeStruct((peers * pitch, LANES), BF16),
            jax.ShapeDtypeStruct(route.shape, jnp.int32),
        ),
        in_specs=[
            pl.BlockSpec(memory_space=pltpu.SMEM),
            pl.BlockSpec(memory_space=pltpu.VMEM),
        ],
        out_specs=(
            pl.BlockSpec(memory_space=pltpu.VMEM),
            pl.BlockSpec(memory_space=pltpu.SMEM),
        ),
        scratch_shapes=[
            pltpu.VMEM(((row_count + 1) * pitch, LANES), F32),
            pltpu.VMEM(((row_count + 1) * pitch, LANES), F32),
            pltpu.SMEM((2 * peers,), jnp.int32),
        ],
        compiler_params=pltpu.CompilerParams(vmem_limit_bytes=16 * 2**20),
        name="pack",
    )(route, tokens)


UP_TILE = 256
DOWN_TILE = 512


def ffn_kernel(
    got_ref, gate_up_ref, down_ref, out_ref, raw, wide, rows, gate_up, down, active, got_sem, up_sem, down_sem
):
    width = rows.shape[1]
    hidden = active.shape[1]
    chunks = width // LANES
    pitch = 2 * chunks
    peers = raw.shape[0] // pitch
    up_steps = hidden // UP_TILE
    down_steps = width // DOWN_TILE

    def up_copy(n):
        half, step = n % 2, n // 2
        return pltpu.make_async_copy(
            gate_up_ref.at[0, :, pl.ds(half * hidden + step * UP_TILE, UP_TILE)],
            gate_up.at[n],
            up_sem.at[n],
        )

    def down_copy(n):
        return pltpu.make_async_copy(
            down_ref.at[0, :, pl.ds(n * DOWN_TILE, DOWN_TILE)], down.at[n], down_sem.at[n]
        )

    got = pltpu.make_async_copy(got_ref, raw, got_sem)
    got.start()
    for n in range(2 * up_steps):
        up_copy(n).start()
    for n in range(down_steps):
        down_copy(n).start()
    got.wait()

    piece = 512

    def widen(i, _):
        span = pl.ds(pl.multiple_of(i * piece, piece), piece)
        wide[span, :] = raw[span, :].astype(F32)
        return 0

    lax.fori_loop(0, peers * pitch // piece, widen, 0)
    for c in range(chunks):
        for r in range(2):
            rows[r * peers : (r + 1) * peers, c * LANES : (c + 1) * LANES] = wide[
                pl.ds(2 * c + r, peers, stride=pitch), :
            ].astype(BF16)

    for step in range(up_steps):
        up_copy(2 * step).wait()
        gate = jnp.dot(rows[...], gate_up[2 * step], preferred_element_type=F32)
        up_copy(2 * step + 1).wait()
        up = jnp.dot(rows[...], gate_up[2 * step + 1], preferred_element_type=F32)
        active[:, step * UP_TILE : (step + 1) * UP_TILE] = (gate / (1 + jnp.exp(-gate)) * up).astype(BF16)

    for step in range(down_steps):
        down_copy(step).wait()
        result = jnp.dot(active[...], down[step], preferred_element_type=F32)
        for q in range(DOWN_TILE // LANES):
            c = step * (DOWN_TILE // LANES) + q
            for r in range(2):
                wide[pl.ds(2 * c + r, peers, stride=pitch), :] = result[
                    r * peers : (r + 1) * peers, q * LANES : (q + 1) * LANES
                ]

    def narrow(i, _):
        span = pl.ds(pl.multiple_of(i * piece, piece), piece)
        out_ref[span, :] = wide[span, :].astype(BF16)
        return 0

    lax.fori_loop(0, peers * pitch // piece, narrow, 0)


def expert_ffn(got, gate_up, down):
    _, width, both = gate_up.shape
    hidden = both // 2
    total = got.shape[0]
    slots = total * LANES // width
    up_steps = 2 * hidden // UP_TILE
    down_steps = width // DOWN_TILE
    return pl.pallas_call(
        ffn_kernel,
        out_shape=jax.ShapeDtypeStruct(got.shape, BF16),
        in_specs=[pl.BlockSpec(memory_space=pl.ANY)] * 3,
        out_specs=pl.BlockSpec(memory_space=pltpu.VMEM),
        scratch_shapes=[
            pltpu.VMEM((total, LANES), BF16),
            pltpu.VMEM((total, LANES), F32),
            pltpu.VMEM((slots, width), BF16),
            pltpu.VMEM((up_steps, width, UP_TILE), BF16),
            pltpu.VMEM((down_steps, hidden, DOWN_TILE), BF16),
            pltpu.VMEM((slots, hidden), BF16),
            pltpu.SemaphoreType.DMA,
            pltpu.SemaphoreType.DMA((up_steps,)),
            pltpu.SemaphoreType.DMA((down_steps,)),
        ],
        compiler_params=pltpu.CompilerParams(vmem_limit_bytes=44 * 2**20),
        cost_estimate=pl.CostEstimate(
            flops=2 * slots * width * hidden * 3, bytes_accessed=6 * width * hidden, transcendentals=slots * hidden
        ),
        name="expert_ffn",
    )(got, gate_up, down)


def combine_kernel(route_ref, rank_ref, weight_ref, got_ref, out_ref, wide, total):
    top_count, row_count = route_ref.shape
    chunks = out_ref.shape[1] // LANES
    pitch = 2 * chunks
    peers = got_ref.shape[0] // pitch
    piece = 512

    def widen(i, _):
        span = pl.ds(pl.multiple_of(i * piece, piece), piece)
        wide[span, :] = got_ref[span, :].astype(F32)
        return 0

    lax.fori_loop(0, peers * pitch // piece, widen, 0)
    parity = lax.broadcasted_iota(jnp.int32, (8, LANES), 0) % 2

    def add_up(t, _):
        acc = jnp.zeros((pitch // 8, 8, LANES), F32)
        for k in range(top_count):
            start = pl.multiple_of(route_ref[k, t] * pitch, 8)
            scale = jnp.where(parity == rank_ref[k, t], weight_ref[k, t], 0.0)
            acc += wide[pl.ds(start, pitch), :].reshape(pitch // 8, 8, LANES) * scale[None]
        total[pl.ds(pl.multiple_of(t * pitch, 8), pitch), :] = acc.reshape(pitch, LANES)
        return 0

    lax.fori_loop(0, row_count, add_up, 0)
    for c in range(chunks):
        out_ref[:, c * LANES : (c + 1) * LANES] = (
            total[pl.ds(2 * c, row_count, stride=pitch), :] + total[pl.ds(2 * c + 1, row_count, stride=pitch), :]
        ).astype(BF16)


def combine(route, rank, weight, got, width):
    row_count = route.shape[1]
    pitch = 2 * width // LANES
    smem = pl.BlockSpec(memory_space=pltpu.SMEM)
    vmem = pl.BlockSpec(memory_space=pltpu.VMEM)
    return pl.pallas_call(
        combine_kernel,
        out_shape=jax.ShapeDtypeStruct((row_count, width), BF16),
        in_specs=[smem, smem, smem, vmem],
        out_specs=vmem,
        scratch_shapes=[
            pltpu.VMEM(got.shape, F32),
            pltpu.VMEM((row_count * pitch, LANES), F32),
        ],
        compiler_params=pltpu.CompilerParams(vmem_limit_bytes=24 * 2**20),
        name="combine",
    )(route, rank, weight, got)


def exchange(blocks, peers):
    shape = blocks.shape
    blocks = blocks.reshape(peers, -1, LANES)
    return lax.all_to_all(blocks, ("node", "local"), split_axis=0, concat_axis=0, tiled=True).reshape(shape)


def on_device(tokens, route, combine_weight, gate_up, down):
    width = tokens.shape[1]
    peers = lax.axis_size("node") * lax.axis_size("local")
    route = route.T
    weight = combine_weight.T.astype(F32)
    send, rank = pack(route, tokens, peers)
    got = exchange(send, peers)
    result = expert_ffn(got, gate_up, down)
    back = exchange(result, peers)
    return combine(route, rank, weight, back, width)


def solution(mesh):
    spec = P(("node", "local"), None)
    weights = P(("node", "local"), None, None)
    return jax.shard_map(
        on_device,
        mesh=mesh,
        in_specs=(spec, spec, spec, weights, weights),
        out_specs=spec,
        check_vma=False,
    )
```

time: 98.5 us -> 92.4 us (0.938)
  Pallas kernels: 0 us -> 20.8 us
  matrix products: 14.3 us -> 0 us
  local copies, waits for them, and re-layouts: 10.4 us -> 1.6 us
  other arithmetic: 3.87 us -> 0.01 us
    pallas_call x0 -> x3, Pallas kernels: none -> 20.8 us  [the longest x1 15.3 us: expert_ffn(): pl.pallas_call(ffn_kernel, out_shape=jax.ShapeDtypeStruct(got.shape, BF16...]
    dot_general x3 -> x0, matrix products: 14.3 us -> none  [the longest x1 7.77 us: expert_rows(): hidden = jnp.dot(rows, gate_up, preferred_element_type=jnp.float32)]
    gather x3 -> x0, local copies, waits for them, and re-layouts: 5.73 us -> none  [the longest x2 3.4 us: on_device(): tokens[fill_source]]
    reshape x3 -> x0, local copies, waits for them, and re-layouts: 3.44 us -> none  [the longest x1 1.69 us: on_device(): results = results.reshape(lead_shape + (model_width,))]
    select_n x5 -> x0, other arithmetic: 3.28 us -> none  [the longest x1 3.26 us: on_device(): jnp.where(slot_live[:, None], tokens[fill_source], jnp.zeros((), jnp.bflo...]
where the time goes in v1:
time: 92.4 us; the launch traced here: 92.2 us
  blocking collectives  38 us (41%)
  waiting for transfers between devices  27.1 us (29%)
  Pallas kernels  20.8 us (23%)
  starting transfers between devices  4.66 us (5%)
  local copies, waits for them, and re-layouts  1.6 us (2%)
    all_to_all x1, blocking collectives, exchange(): lax.all_to_all(blocks, ('node', 'local'), split_axis=0, concat_axis=0, ti...  38 us
    all_to_all x1, waiting for transfers between devices, exchange(): lax.all_to_all(blocks, ('node', 'local'), split_axis=0, concat_axis=0, ti...  27.1 us
    pallas_call x1, Pallas kernels, expert_ffn(): pl.pallas_call(ffn_kernel, out_shape=jax.ShapeDtypeStruct(got.shape, BF16...  15.3 us
    all_to_all x1, starting transfers between devices, exchange(): lax.all_to_all(blocks, ('node', 'local'), split_axis=0, concat_axis=0, ti...  4.66 us
    pallas_call x1, Pallas kernels, pack(): pl.pallas_call(pack_kernel, out_shape=(jax.ShapeDtypeStruct((peers * pitc...  3.25 us
    pallas_call x1, Pallas kernels, combine(): pl.pallas_call(combine_kernel, out_shape=jax.ShapeDtypeStruct((row_count,...  2.21 us
  transfers between devices with their start and end apart: 1, of which 1 were waited for; matrix products, arithmetic and copies ran while one was open for 0% of the time, Pallas kernels for 0%

profile of v1, /device:TPU:0, one launch (start us, length us, event | category | flops | bytes accessed | tf_op | source)
XLA Modules:
  0.0 92.2 jit_solution(1877811268443966870)
XLA Ops:
  0.0 0.0 copy-start
  0.0 0.9 copy-done
  0.9 0.0 copy-start.1
  0.9 0.7 copy-done.1
  1.6 3.3 %pack.1 = (bf16[7168,128]{1,0:T(8,128)(2,1)S(1)}, s32[8,16]{1,0:T(8,128)S(1)}) custom-call(s32[8,16]{1,0:T(8,128)S(1)} %bitcast.10, bf16[16,3584]{1,0:T(8,128)(2,1)S(1)} %copy-done), custom_call_target="tpu_custom_call" | custom-call | tf_op jit(solution)/shard_map/pack/pallas_call | solution.py:61
  4.8 38.0 %all_to_all.10 = bf16[128,56,128]{2,1,0:T(8,128)(2,1)S(1)} all-to-all(bf16[128,56,128]{2,1,0:T(8,128)(2,1)S(1)} %bitcast.9), channel_id=1, replica_groups=mesh['node'=8,'local'=16] {'node','local'}, dimensions={0} | all-to-all | bytes 3670016 | tf_op jit(solution)/shard_map/all_to_all | solution.py:244
  42.9 15.3 %expert_ffn.1 = bf16[7168,128]{1,0:T(8,128)(2,1)} custom-call(bf16[7168,128]{1,0:T(8,128)(2,1)S(1)} %bitcast.7, bf16[1,3584,2048]{2,1,0:T(8,128)(2,1)} %gate_up_ref.1, bf16[1,1024,3584]{2,1,0:T(8,128)(2,1)} %down_ref.1), custom_call_target="tpu_custom_call" | custom-call | flops 5637144576 | bytes 22020096 | tf_op jit(solution)/shard_map/expert_ffn/pallas_call | solution.py:167
  58.2 0.0 copy-start.3
  58.2 0.0 copy-start.2
  58.2 4.7 %all-to-all-start.1 = ((bf16[128,56,128]{2,1,0:T(8,128)(2,1)}), bf16[128,56,128]{2,1,0:T(8,128)(2,1)S(1)}, u32[]{:S(2)}, u32[]{:S(2)}) async-start(bf16[128,56,128]{2,1,0:T(8,128)(2,1)} %bitcast.4), calls=%async_computation.1 | async-start | bytes 3670016 | tf_op jit(solution)/shard_map/all_to_all | solution.py:244
  62.9 0.0 copy-done.3
  62.9 27.1 %all-to-all-done.1 = bf16[128,56,128]{2,1,0:T(8,128)(2,1)S(1)} async-done(((bf16[128,56,128]{2,1,0:T(8,128)(2,1)}), bf16[128,56,128]{2,1,0:T(8,128)(2,1)S(1)}, u32[]{:S(2)}, u32[]{:S(2)}) %all-to-all-start.1) | async-done | bytes 1835040 | tf_op jit(solution)/shard_map/all_to_all | solution.py:244
  89.9 0.0 copy-done.2
  90.0 2.2 %combine.1 = bf16[16,3584]{1,0:T(8,128)(2,1)} custom-call(s32[8,16]{1,0:T(8,128)S(1)} %bitcast.11, s32[8,16]{1,0:T(8,128)S(1)} %get-tuple-element.7.rank_ref, f32[8,16]{1,0:T(8,128)S(1)} %convert_bitcast_fusion.weight_ref, bf16[7168,128]{1,0:T(8,128)(2,1)S(1)} %bitcast.8), custom_call_target="tpu_custom_call" | custom-call | tf_op jit(solution)/shard_map/combine/pallas_call | solution.py:227
  (1 shorter events, 0.0 us)
Async XLA Ops:
  0.0 0.9 copy-start
  0.9 0.7 copy-start.1
  58.2 4.7 %copy-start.3 = (bf16[16,8]{0,1:T(8,128)(2,1)S(1)}, bf16[16,8]{0,1:T(8,128)(2,1)}, u32[]{:S(2)}) copy-start(bf16[16,8]{0,1:T(8,128)(2,1)} %param.7) | copy-start | bytes 772
  58.2 31.8 %copy-start.2 = (s32[16,8]{0,1:T(8,128)S(1)}, s32[16,8]{0,1:T(8,128)}, u32[]{:S(2)}) copy-start(s32[16,8]{0,1:T(8,128)} %param.6) | copy-start | bytes 1540
  58.2 31.7 %all-to-all-start.1 = ((bf16[128,56,128]{2,1,0:T(8,128)(2,1)}), bf16[128,56,128]{2,1,0:T(8,128)(2,1)S(1)}, u32[]{:S(2)}, u32[]{:S(2)}) async-start(bf16[128,56,128]{2,1,0:T(8,128)(2,1)} %bitcast.4), calls=%async_computation.1 | async-start | bytes 3670016 | tf_op jit(solution)/shard_map/all_to_all | solution.py:244

commit v2 on v1

--- a/solution.py
+++ b/solution.py
@@ -1,5 +1,3 @@
-import functools
-
 import jax
 import jax.numpy as jnp
 from jax import lax
@@ -84,48 +82,48 @@
 
 UP_TILE = 256
 DOWN_TILE = 512
-
-
-def ffn_kernel(
-    got_ref, gate_up_ref, down_ref, out_ref, raw, wide, rows, gate_up, down, active, got_sem, up_sem, down_sem
-):
+DOWN_GROUP = 4
+IN_FLIGHT = 6
+PIECE = 512
+
+
+def ffn_kernel(got_ref, gate_up_ref, down_ref, out_ref, wide, rows, gate_up, down, active, up_sem, down_sem):
     width = rows.shape[1]
     hidden = active.shape[1]
     chunks = width // LANES
     pitch = 2 * chunks
-    peers = raw.shape[0] // pitch
+    peers = got_ref.shape[0] // pitch
     up_steps = hidden // UP_TILE
     down_steps = width // DOWN_TILE
 
-    def up_copy(n):
-        half, step = n % 2, n // 2
-        return pltpu.make_async_copy(
-            gate_up_ref.at[0, :, pl.ds(half * hidden + step * UP_TILE, UP_TILE)],
-            gate_up.at[n],
-            up_sem.at[n],
+    copies = []
+    for n in range(2 * up_steps):
+        start = n % 2 * hidden + n // 2 * UP_TILE
+        copies.append(
+            pltpu.make_async_copy(
+                gate_up_ref.at[0, :, pl.ds(start, UP_TILE)], gate_up.at[n], up_sem.at[n]
+            )
         )
-
-    def down_copy(n):
-        return pltpu.make_async_copy(
-            down_ref.at[0, :, pl.ds(n * DOWN_TILE, DOWN_TILE)], down.at[n], down_sem.at[n]
+    for n in range(down_steps):
+        copies.append(
+            pltpu.make_async_copy(
+                down_ref.at[0, :, pl.ds(n * DOWN_TILE, DOWN_TILE)], down.at[n], down_sem.at[n]
+            )
         )
-
-    got = pltpu.make_async_copy(got_ref, raw, got_sem)
-    got.start()
-    for n in range(2 * up_steps):
-        up_copy(n).start()
-    for n in range(down_steps):
-        down_copy(n).start()
-    got.wait()
-
-    piece = 512
+    for copy in copies[:IN_FLIGHT]:
+        copy.start()
+
+    def take(n):
+        copies[n].wait()
+        if n + IN_FLIGHT < len(copies):
+            copies[n + IN_FLIGHT].start()
 
     def widen(i, _):
-        span = pl.ds(pl.multiple_of(i * piece, piece), piece)
-        wide[span, :] = raw[span, :].astype(F32)
-        return 0
-
-    lax.fori_loop(0, peers * pitch // piece, widen, 0)
+        span = pl.ds(pl.multiple_of(i * PIECE, PIECE), PIECE)
+        wide[span, :] = got_ref[span, :].astype(F32)
+        return 0
+
+    lax.fori_loop(0, peers * pitch // PIECE, widen, 0)
     for c in range(chunks):
         for r in range(2):
             rows[r * peers : (r + 1) * peers, c * LANES : (c + 1) * LANES] = wide[
@@ -133,28 +131,31 @@
             ].astype(BF16)
 
     for step in range(up_steps):
-        up_copy(2 * step).wait()
+        take(2 * step)
+        take(2 * step + 1)
         gate = jnp.dot(rows[...], gate_up[2 * step], preferred_element_type=F32)
-        up_copy(2 * step + 1).wait()
         up = jnp.dot(rows[...], gate_up[2 * step + 1], preferred_element_type=F32)
         active[:, step * UP_TILE : (step + 1) * UP_TILE] = (gate / (1 + jnp.exp(-gate)) * up).astype(BF16)
 
-    for step in range(down_steps):
-        down_copy(step).wait()
-        result = jnp.dot(active[...], down[step], preferred_element_type=F32)
-        for q in range(DOWN_TILE // LANES):
-            c = step * (DOWN_TILE // LANES) + q
-            for r in range(2):
-                wide[pl.ds(2 * c + r, peers, stride=pitch), :] = result[
-                    r * peers : (r + 1) * peers, q * LANES : (q + 1) * LANES
-                ]
+    for first in range(0, down_steps, DOWN_GROUP):
+        steps = range(first, min(first + DOWN_GROUP, down_steps))
+        for step in steps:
+            take(2 * up_steps + step)
+        for step in steps:
+            result = jnp.dot(active[...], down[step], preferred_element_type=F32)
+            for q in range(DOWN_TILE // LANES):
+                c = step * (DOWN_TILE // LANES) + q
+                for r in range(2):
+                    wide[pl.ds(2 * c + r, peers, stride=pitch), :] = result[
+                        r * peers : (r + 1) * peers, q * LANES : (q + 1) * LANES
+                    ]
 
     def narrow(i, _):
-        span = pl.ds(pl.multiple_of(i * piece, piece), piece)
+        span = pl.ds(pl.multiple_of(i * PIECE, PIECE), PIECE)
         out_ref[span, :] = wide[span, :].astype(BF16)
         return 0
 
-    lax.fori_loop(0, peers * pitch // piece, narrow, 0)
+    lax.fori_loop(0, peers * pitch // PIECE, narrow, 0)
 
 
 def expert_ffn(got, gate_up, down):
@@ -162,23 +163,25 @@
     hidden = both // 2
     total = got.shape[0]
     slots = total * LANES // width
-    up_steps = 2 * hidden // UP_TILE
-    down_steps = width // DOWN_TILE
+    up_tiles = both // UP_TILE
+    down_tiles = width // DOWN_TILE
     return pl.pallas_call(
         ffn_kernel,
         out_shape=jax.ShapeDtypeStruct(got.shape, BF16),
-        in_specs=[pl.BlockSpec(memory_space=pl.ANY)] * 3,
+        in_specs=[
+            pl.BlockSpec(memory_space=pltpu.VMEM),
+            pl.BlockSpec(memory_space=pl.ANY),
+            pl.BlockSpec(memory_space=pl.ANY),
+        ],
         out_specs=pl.BlockSpec(memory_space=pltpu.VMEM),
         scratch_shapes=[
-            pltpu.VMEM((total, LANES), BF16),
             pltpu.VMEM((total, LANES), F32),
             pltpu.VMEM((slots, width), BF16),
-            pltpu.VMEM((up_steps, width, UP_TILE), BF16),
-            pltpu.VMEM((down_steps, hidden, DOWN_TILE), BF16),
+            pltpu.VMEM((up_tiles, width, UP_TILE), BF16),
+            pltpu.VMEM((down_tiles, hidden, DOWN_TILE), BF16),
             pltpu.VMEM((slots, hidden), BF16),
-            pltpu.SemaphoreType.DMA,
-            pltpu.SemaphoreType.DMA((up_steps,)),
-            pltpu.SemaphoreType.DMA((down_steps,)),
+            pltpu.SemaphoreType.DMA((up_tiles,)),
+            pltpu.SemaphoreType.DMA((down_tiles,)),
         ],
         compiler_params=pltpu.CompilerParams(vmem_limit_bytes=44 * 2**20),
         cost_estimate=pl.CostEstimate(
@@ -193,14 +196,12 @@
     chunks = out_ref.shape[1] // LANES
     pitch = 2 * chunks
     peers = got_ref.shape[0] // pitch
-    piece = 512
-
     def widen(i, _):
-        span = pl.ds(pl.multiple_of(i * piece, piece), piece)
+        span = pl.ds(pl.multiple_of(i * PIECE, PIECE), PIECE)
         wide[span, :] = got_ref[span, :].astype(F32)
         return 0
 
-    lax.fori_loop(0, peers * pitch // piece, widen, 0)
+    lax.fori_loop(0, peers * pitch // PIECE, widen, 0)
     parity = lax.broadcasted_iota(jnp.int32, (8, LANES), 0) % 2
 
     def add_up(t, _):

time: 92.4 us -> 87.9 us (0.951)
  Pallas kernels: 20.8 us -> 16.3 us
    pallas_call x1, Pallas kernels: 15.3 us -> 10.8 us  [expert_ffn(): pl.pallas_call(ffn_kernel, out_shape=jax.ShapeDtypeStruct(got.shape, BF16...]
where the time goes in v2:
time: 87.9 us; the launch traced here: 87.7 us
  blocking collectives  38 us (43%)
  waiting for transfers between devices  27.1 us (31%)
  Pallas kernels  16.3 us (19%)
  starting transfers between devices  4.66 us (5%)
  local copies, waits for them, and re-layouts  1.6 us (2%)
    all_to_all x1, blocking collectives, exchange(): lax.all_to_all(blocks, ('node', 'local'), split_axis=0, concat_axis=0, ti...  38 us
    all_to_all x1, waiting for transfers between devices, exchange(): lax.all_to_all(blocks, ('node', 'local'), split_axis=0, concat_axis=0, ti...  27.1 us
    pallas_call x1, Pallas kernels, expert_ffn(): pl.pallas_call(ffn_kernel, out_shape=jax.ShapeDtypeStruct(got.shape, BF16...  10.8 us
    all_to_all x1, starting transfers between devices, exchange(): lax.all_to_all(blocks, ('node', 'local'), split_axis=0, concat_axis=0, ti...  4.66 us
    pallas_call x1, Pallas kernels, pack(): pl.pallas_call(pack_kernel, out_shape=(jax.ShapeDtypeStruct((peers * pitc...  3.25 us
    pallas_call x1, Pallas kernels, combine(): pl.pallas_call(combine_kernel, out_shape=jax.ShapeDtypeStruct((row_count,...  2.21 us
  transfers between devices with their start and end apart: 1, of which 1 were waited for; matrix products, arithmetic and copies ran while one was open for 0% of the time, Pallas kernels for 0%

profile of v2, /device:TPU:0, one launch (start us, length us, event | category | flops | bytes accessed | tf_op | source)
XLA Modules:
  0.0 87.7 jit_solution(8655484559849656670)
XLA Ops:
  0.0 0.0 copy-start
  0.0 0.9 %copy-done = bf16[16,3584]{1,0:T(8,128)(2,1)S(1)} copy-done((bf16[16,3584]{1,0:T(8,128)(2,1)S(1)}, bf16[16,3584]{1,0:T(8,128)(2,1)}, u32[]{:S(2)}) %copy-start) | copy-done | bytes 114712
  0.9 0.0 copy-start.1
  0.9 0.7 copy-done.1
  1.6 3.3 %pack.1 = (bf16[7168,128]{1,0:T(8,128)(2,1)S(1)}, s32[8,16]{1,0:T(8,128)S(1)}) custom-call(s32[8,16]{1,0:T(8,128)S(1)} %bitcast.10, bf16[16,3584]{1,0:T(8,128)(2,1)S(1)} %copy-done), custom_call_target="tpu_custom_call" | custom-call | tf_op jit(solution)/shard_map/pack/pallas_call | solution.py:59
  4.8 38.0 %all_to_all.10 = bf16[128,56,128]{2,1,0:T(8,128)(2,1)S(1)} all-to-all(bf16[128,56,128]{2,1,0:T(8,128)(2,1)S(1)} %bitcast.9), channel_id=1, replica_groups=mesh['node'=8,'local'=16] {'node','local'}, dimensions={0} | all-to-all | bytes 3670016 | tf_op jit(solution)/shard_map/all_to_all | solution.py:245
  42.9 10.8 %expert_ffn.1 = bf16[7168,128]{1,0:T(8,128)(2,1)} custom-call(bf16[7168,128]{1,0:T(8,128)(2,1)S(1)} %bitcast.7, bf16[1,3584,2048]{2,1,0:T(8,128)(2,1)} %gate_up_ref.1, bf16[1,1024,3584]{2,1,0:T(8,128)(2,1)} %down_ref.1), custom_call_target="tpu_custom_call" | custom-call | flops 5637144576 | bytes 22020096 | tf_op jit(solution)/shard_map/expert_ffn/pallas_call | solution.py:168
  53.7 0.0 copy-start.3
  53.7 0.0 copy-start.2
  53.7 4.7 %all-to-all-start.1 = ((bf16[128,56,128]{2,1,0:T(8,128)(2,1)}), bf16[128,56,128]{2,1,0:T(8,128)(2,1)S(1)}, u32[]{:S(2)}, u32[]{:S(2)}) async-start(bf16[128,56,128]{2,1,0:T(8,128)(2,1)} %bitcast.4), calls=%async_computation.1 | async-start | bytes 3670016 | tf_op jit(solution)/shard_map/all_to_all | solution.py:245
  58.4 0.0 copy-done.3
  58.4 27.1 %all-to-all-done.1 = bf16[128,56,128]{2,1,0:T(8,128)(2,1)S(1)} async-done(((bf16[128,56,128]{2,1,0:T(8,128)(2,1)}), bf16[128,56,128]{2,1,0:T(8,128)(2,1)S(1)}, u32[]{:S(2)}, u32[]{:S(2)}) %all-to-all-start.1) | async-done | bytes 1835040 | tf_op jit(solution)/shard_map/all_to_all | solution.py:245
  85.5 0.0 copy-done.2
  85.5 2.2 %combine.1 = bf16[16,3584]{1,0:T(8,128)(2,1)} custom-call(s32[8,16]{1,0:T(8,128)S(1)} %bitcast.11, s32[8,16]{1,0:T(8,128)S(1)} %get-tuple-element.7.rank_ref, f32[8,16]{1,0:T(8,128)S(1)} %convert_bitcast_fusion.weight_ref, bf16[7168,128]{1,0:T(8,128)(2,1)S(1)} %bitcast.8), custom_call_target="tpu_custom_call" | custom-call | tf_op jit(solution)/shard_map/combine/pallas_call | solution.py:228
  (1 shorter events, 0.0 us)
Async XLA Ops:
  0.0 0.9 %copy-start = (bf16[16,3584]{1,0:T(8,128)(2,1)S(1)}, bf16[16,3584]{1,0:T(8,128)(2,1)}, u32[]{:S(2)}) copy-start(bf16[16,3584]{1,0:T(8,128)(2,1)} %tokens_ref.1) | copy-start | bytes 344068
  0.9 0.7 copy-start.1
  53.7 4.7 %copy-start.3 = (bf16[16,8]{0,1:T(8,128)(2,1)S(1)}, bf16[16,8]{0,1:T(8,128)(2,1)}, u32[]{:S(2)}) copy-start(bf16[16,8]{0,1:T(8,128)(2,1)} %param.7) | copy-start | bytes 772
  53.7 31.8 %copy-start.2 = (s32[16,8]{0,1:T(8,128)S(1)}, s32[16,8]{0,1:T(8,128)}, u32[]{:S(2)}) copy-start(s32[16,8]{0,1:T(8,128)} %param.6) | copy-start | bytes 1540
  53.7 31.7 %all-to-all-start.1 = ((bf16[128,56,128]{2,1,0:T(8,128)(2,1)}), bf16[128,56,128]{2,1,0:T(8,128)(2,1)S(1)}, u32[]{:S(2)}, u32[]{:S(2)}) async-start(bf16[128,56,128]{2,1,0:T(8,128)(2,1)} %bitcast.4), calls=%async_computation.1 | async-start | bytes 3670016 | tf_op jit(solution)/shard_map/all_to_all | solution.py:245

commit v3 on v2

--- a/solution.py
+++ b/solution.py
@@ -10,72 +10,95 @@
 BF16 = jnp.bfloat16
 
 
-def pack_kernel(route_ref, tokens_ref, out_ref, rank_ref, low, high, source):
-    top_count, row_count = route_ref.shape
-    chunks = tokens_ref.shape[1] // LANES
+PACK_STEPS = 8
+
+
+def pack_kernel(
+    route_ref, tokens_ref, out_ref, first_ref, route, tokens, blocks, first, low, high, source, in_sem, out_sem
+):
+    top_count, row_count = route.shape
+    chunks = tokens.shape[1] // LANES
     pitch = 2 * chunks
-    peers = out_ref.shape[0] // pitch
-
+    peers = blocks.shape[0] // pitch
+    step_peers = peers // PACK_STEPS
+
+    fetch_route = pltpu.make_async_copy(route_ref, route, in_sem.at[0])
+    fetch_tokens = pltpu.make_async_copy(tokens_ref, tokens, in_sem.at[1])
+    fetch_route.start()
+    fetch_tokens.start()
     low[...] = jnp.zeros_like(low)
     high[...] = jnp.zeros_like(high)
+    fetch_route.wait()
+
+    peer = lax.broadcasted_iota(jnp.int32, (top_count, peers), 1)
+    lowest = jnp.full((top_count, peers), row_count, jnp.int32)
+    highest = jnp.full((top_count, peers), -1, jnp.int32)
+    for t in range(row_count):
+        named = route[:, t : t + 1] == peer
+        lowest = jnp.where(named, jnp.minimum(lowest, t), lowest)
+        highest = jnp.where(named, t, highest)
+    lowest = jnp.min(lowest, axis=0, keepdims=True)
+    highest = jnp.max(highest, axis=0, keepdims=True)
+    second = jnp.where(highest > lowest, highest, row_count)
+    side = lax.broadcasted_iota(jnp.int32, (8, peers), 0)
+    first[...] = jnp.where(side == 0, lowest, second)
+    publish = pltpu.make_async_copy(first, source, in_sem.at[2])
+    publish.start()
+    keep = pltpu.make_async_copy(first, first_ref, in_sem.at[3])
+    keep.start()
+    fetch_tokens.wait()
     for c in range(chunks):
-        part = tokens_ref[:, c * LANES : (c + 1) * LANES].astype(F32)
+        part = tokens[:, c * LANES : (c + 1) * LANES].astype(F32)
         low[pl.ds(2 * c, row_count, stride=pitch), :] = part
         high[pl.ds(2 * c + 1, row_count, stride=pitch), :] = part
-
-    def clear(i, _):
-        source[i] = row_count
-        return 0
-
-    lax.fori_loop(0, 2 * peers, clear, 0, unroll=16)
-
-    def place(t, _):
-        for k in range(top_count):
-            e = route_ref[k, t]
-            r = jnp.where(source[e] == row_count, 0, 1)
-            source[r * peers + e] = t
-            rank_ref[k, t] = r
-        return 0
-
-    lax.fori_loop(0, row_count, place, 0)
+    publish.wait()
 
     def fill(i, _):
-        blocks = []
+        pair = []
         for p in (2 * i, 2 * i + 1):
-            a = pl.multiple_of(source[p] * pitch, 8)
-            b = pl.multiple_of(source[peers + p] * pitch, 8)
-            blocks.append(low[pl.ds(a, pitch), :] + high[pl.ds(b, pitch), :])
-        out_ref[pl.ds(pl.multiple_of(i * 2 * pitch, 16), 2 * pitch), :] = jnp.concatenate(
-            blocks, axis=0
+            a = pl.multiple_of(source[0, p] * pitch, 8)
+            b = pl.multiple_of(source[1, p] * pitch, 8)
+            pair.append(low[pl.ds(a, pitch), :] + high[pl.ds(b, pitch), :])
+        blocks[pl.ds(pl.multiple_of(i * 2 * pitch, 16), 2 * pitch), :] = jnp.concatenate(
+            pair, axis=0
         ).astype(BF16)
         return 0
 
-    lax.fori_loop(0, peers // 2, fill, 0, unroll=2)
+    sends = []
+    for step in range(PACK_STEPS):
+        lax.fori_loop(step * step_peers // 2, (step + 1) * step_peers // 2, fill, 0, unroll=4)
+        span = pl.ds(step * step_peers * pitch, step_peers * pitch)
+        sends.append(pltpu.make_async_copy(blocks.at[span], out_ref.at[span], out_sem.at[step]))
+        sends[step].start()
+    keep.wait()
+    for send in sends:
+        send.wait()
 
 
 def pack(route, tokens, peers):
     row_count, width = tokens.shape
     pitch = 2 * width // LANES
+    anywhere = pl.BlockSpec(memory_space=pl.ANY)
     return pl.pallas_call(
         pack_kernel,
         out_shape=(
             jax.ShapeDtypeStruct((peers * pitch, LANES), BF16),
-            jax.ShapeDtypeStruct(route.shape, jnp.int32),
+            jax.ShapeDtypeStruct((8, peers), jnp.int32),
         ),
-        in_specs=[
-            pl.BlockSpec(memory_space=pltpu.SMEM),
-            pl.BlockSpec(memory_space=pltpu.VMEM),
-        ],
-        out_specs=(
-            pl.BlockSpec(memory_space=pltpu.VMEM),
-            pl.BlockSpec(memory_space=pltpu.SMEM),
-        ),
+        in_specs=[anywhere, anywhere],
+        out_specs=(anywhere, anywhere),
         scratch_shapes=[
+            pltpu.VMEM(route.shape, jnp.int32),
+            pltpu.VMEM(tokens.shape, BF16),
+            pltpu.VMEM((peers * pitch, LANES), BF16),
+            pltpu.VMEM((8, peers), jnp.int32),
             pltpu.VMEM(((row_count + 1) * pitch, LANES), F32),
             pltpu.VMEM(((row_count + 1) * pitch, LANES), F32),
-            pltpu.SMEM((2 * peers,), jnp.int32),
+            pltpu.SMEM((8, peers), jnp.int32),
+            pltpu.SemaphoreType.DMA((4,)),
+            pltpu.SemaphoreType.DMA((PACK_STEPS,)),
         ],
-        compiler_params=pltpu.CompilerParams(vmem_limit_bytes=16 * 2**20),
+        compiler_params=pltpu.CompilerParams(vmem_limit_bytes=60000000),
         name="pack",
     )(route, tokens)
 
@@ -191,52 +214,79 @@
     )(got, gate_up, down)
 
 
-def combine_kernel(route_ref, rank_ref, weight_ref, got_ref, out_ref, wide, total):
-    top_count, row_count = route_ref.shape
+def combine_kernel(
+    route_ref, first_ref, weight_ref, got_ref, out_ref, wide, total, narrow, scale, route, first, weight, sem
+):
+    top_count, row_count = route.shape
     chunks = out_ref.shape[1] // LANES
     pitch = 2 * chunks
     peers = got_ref.shape[0] // pitch
+
+    fetch_weight = pltpu.make_async_copy(weight_ref, narrow, sem.at[0])
+    fetch_route = pltpu.make_async_copy(route_ref, route, sem.at[1])
+    fetch_first = pltpu.make_async_copy(first_ref, first, sem.at[2])
+    fetch_weight.start()
+    fetch_route.start()
+    fetch_first.start()
+
     def widen(i, _):
         span = pl.ds(pl.multiple_of(i * PIECE, PIECE), PIECE)
         wide[span, :] = got_ref[span, :].astype(F32)
         return 0
 
-    lax.fori_loop(0, peers * pitch // PIECE, widen, 0)
+    pieces = peers * pitch // PIECE
+    lax.fori_loop(0, pieces // 2, widen, 0)
+    fetch_weight.wait()
+    scale[...] = narrow[...].astype(F32)
+    publish = pltpu.make_async_copy(scale, weight, sem.at[3])
+    publish.start()
+    lax.fori_loop(pieces // 2, pieces, widen, 0)
+    fetch_route.wait()
+    fetch_first.wait()
+    publish.wait()
     parity = lax.broadcasted_iota(jnp.int32, (8, LANES), 0) % 2
 
     def add_up(t, _):
         acc = jnp.zeros((pitch // 8, 8, LANES), F32)
         for k in range(top_count):
-            start = pl.multiple_of(route_ref[k, t] * pitch, 8)
-            scale = jnp.where(parity == rank_ref[k, t], weight_ref[k, t], 0.0)
-            acc += wide[pl.ds(start, pitch), :].reshape(pitch // 8, 8, LANES) * scale[None]
+            e = route[k, t]
+            start = pl.multiple_of(e * pitch, 8)
+            rank = jnp.where(first[0, e] == t, 0, 1)
+            factor = jnp.where(parity == rank, weight[k, t], 0.0)
+            acc += wide[pl.ds(start, pitch), :].reshape(pitch // 8, 8, LANES) * factor[None]
         total[pl.ds(pl.multiple_of(t * pitch, 8), pitch), :] = acc.reshape(pitch, LANES)
         return 0
 
-    lax.fori_loop(0, row_count, add_up, 0)
+    lax.fori_loop(0, row_count, add_up, 0, unroll=4)
     for c in range(chunks):
         out_ref[:, c * LANES : (c + 1) * LANES] = (
             total[pl.ds(2 * c, row_count, stride=pitch), :] + total[pl.ds(2 * c + 1, row_count, stride=pitch), :]
         ).astype(BF16)
 
 
-def combine(route, rank, weight, got, width):
+def combine(route, first, weight, got, width):
     row_count = route.shape[1]
     pitch = 2 * width // LANES
-    smem = pl.BlockSpec(memory_space=pltpu.SMEM)
+    anywhere = pl.BlockSpec(memory_space=pl.ANY)
     vmem = pl.BlockSpec(memory_space=pltpu.VMEM)
     return pl.pallas_call(
         combine_kernel,
         out_shape=jax.ShapeDtypeStruct((row_count, width), BF16),
-        in_specs=[smem, smem, smem, vmem],
+        in_specs=[anywhere, anywhere, anywhere, vmem],
         out_specs=vmem,
         scratch_shapes=[
             pltpu.VMEM(got.shape, F32),
             pltpu.VMEM((row_count * pitch, LANES), F32),
+            pltpu.VMEM(weight.shape, BF16),
+            pltpu.VMEM(weight.shape, F32),
+            pltpu.SMEM(route.shape, jnp.int32),
+            pltpu.SMEM(first.shape, jnp.int32),
+            pltpu.SMEM(weight.shape, F32),
+            pltpu.SemaphoreType.DMA((4,)),
         ],
         compiler_params=pltpu.CompilerParams(vmem_limit_bytes=24 * 2**20),
         name="combine",
-    )(route, rank, weight, got)
+    )(route, first, weight, got)
 
 
 def exchange(blocks, peers):
@@ -249,12 +299,11 @@
     width = tokens.shape[1]
     peers = lax.axis_size("node") * lax.axis_size("local")
     route = route.T
-    weight = combine_weight.T.astype(F32)
-    send, rank = pack(route, tokens, peers)
+    send, first = pack(route, tokens, peers)
     got = exchange(send, peers)
     result = expert_ffn(got, gate_up, down)
     back = exchange(result, peers)
-    return combine(route, rank, weight, back, width)
+    return combine(route, first, combine_weight.T, back, width)
 
 
 def solution(mesh):

time: 87.9 us -> 84.3 us (0.959)
  blocking collectives: 38 us -> 69.6 us
  waiting for transfers between devices: 27.1 us -> 0 us
  starting transfers between devices: 4.66 us -> 0 us
  Pallas kernels: 16.3 us -> 14.4 us
  local copies, waits for them, and re-layouts: 1.6 us -> 0.02 us
    all_to_all x1 -> x2, blocking collectives: 38 us -> 69.6 us  [exchange(): lax.all_to_all(blocks, ('node', 'local'), split_axis=0, concat_axis=0, ti...]
    all_to_all x1 -> x0, waiting for transfers between devices: 27.1 us -> none  [exchange(): lax.all_to_all(blocks, ('node', 'local'), split_axis=0, concat_axis=0, ti...]
    all_to_all x1 -> x0, starting transfers between devices: 4.66 us -> none  [exchange(): lax.all_to_all(blocks, ('node', 'local'), split_axis=0, concat_axis=0, ti...]
    unnamed x8 -> x6, local copies, waits for them, and re-layouts: 1.6 us -> 0.02 us
    pallas_call x1, Pallas kernels: 10.8 us -> 9.54 us  [expert_ffn(): pl.pallas_call(ffn_kernel, out_shape=jax.ShapeDtypeStruct(got.shape, BF16...]
  transfers between devices with their start and end apart: 1 -> 0, of which waited for: 1 -> 0; matrix products, arithmetic and copies ran while one was open for 0% -> 0% of each run, Pallas kernels for 0% -> 0%
where the time goes in v3:
time: 84.3 us; the launch traced here: 84 us
  blocking collectives  69.6 us (83%)
  Pallas kernels  14.4 us (17%)
    all_to_all x2, blocking collectives, exchange(): lax.all_to_all(blocks, ('node', 'local'), split_axis=0, concat_axis=0, ti...  69.6 us
    pallas_call x1, Pallas kernels, expert_ffn(): pl.pallas_call(ffn_kernel, out_shape=jax.ShapeDtypeStruct(got.shape, BF16...  9.54 us
    pallas_call x1, Pallas kernels, pack(): pl.pallas_call(pack_kernel, out_shape=(jax.ShapeDtypeStruct((peers * pitc...  2.96 us
    pallas_call x1, Pallas kernels, combine(): pl.pallas_call(combine_kernel, out_shape=jax.ShapeDtypeStruct((row_count,...  1.9 us

profile of v3, /device:TPU:0, one launch (start us, length us, event | category | flops | bytes accessed | tf_op | source)
XLA Modules:
  0.0 84.0 jit_solution(4924488715066108561)
XLA Ops:
  0.0 3.0 %pack.1 = (bf16[7168,128]{1,0:T(8,128)(2,1)}, s32[8,128]{1,0:T(8,128)}) custom-call(s32[8,16]{1,0:T(8,128)} %bitcast.9, bf16[16,3584]{1,0:T(8,128)(2,1)} %tokens_ref.1), custom_call_target="tpu_custom_call" | custom-call | tf_op jit(solution)/shard_map/pack/pallas_call | solution.py:82
  3.0 38.2 %all_to_all.10 = bf16[128,56,128]{2,1,0:T(8,128)(2,1)S(1)} all-to-all(bf16[128,56,128]{2,1,0:T(8,128)(2,1)} %bitcast.12), channel_id=1, replica_groups=mesh['node'=8,'local'=16] {'node','local'}, dimensions={0} | all-to-all | bytes 3670016 | tf_op jit(solution)/shard_map/all_to_all | solution.py:295
  41.2 9.5 %expert_ffn.1 = bf16[7168,128]{1,0:T(8,128)(2,1)S(1)} custom-call(bf16[7168,128]{1,0:T(8,128)(2,1)S(1)} %bitcast.6, bf16[1,3584,2048]{2,1,0:T(8,128)(2,1)} %gate_up_ref.1, bf16[1,1024,3584]{2,1,0:T(8,128)(2,1)} %down_ref.1), custom_call_target="tpu_custom_call" | custom-call | flops 5637144576 | bytes 22020096 | tf_op jit(solution)/shard_map/expert_ffn/pallas_call | solution.py:191
  50.8 0.0 copy-start
  50.8 0.0 copy-start.1
  50.8 0.0 copy-start.2
  50.8 31.3 %all_to_all.11 = bf16[128,56,128]{2,1,0:T(8,128)(2,1)S(1)} all-to-all(bf16[128,56,128]{2,1,0:T(8,128)(2,1)S(1)} %bitcast.7), channel_id=1, replica_groups=mesh['node'=8,'local'=16] {'node','local'}, dimensions={0} | all-to-all | bytes 3670016 | tf_op jit(solution)/shard_map/all_to_all | solution.py:295
  82.1 0.0 copy-done
  82.1 0.0 copy-done.1
  82.1 0.0 copy-done.2
  82.1 1.9 %combine.1 = bf16[16,3584]{1,0:T(8,128)(2,1)} custom-call(s32[8,16]{1,0:T(8,128)S(1)} %bitcast.10, s32[8,128]{1,0:T(8,128)S(1)} %copy-done.1, bf16[8,16]{1,0:T(8,128)(2,1)S(1)} %bitcast.11, bf16[7168,128]{1,0:T(8,128)(2,1)S(1)} %bitcast.8), custom_call_target="tpu_custom_call" | custom-call | tf_op jit(solution)/shard_map/combine/pallas_call | solution.py:272
Async XLA Ops:
  50.8 31.4 %copy-start = (s32[16,8]{0,1:T(8,128)S(1)}, s32[16,8]{0,1:T(8,128)}, u32[]{:S(2)}) copy-start(s32[16,8]{0,1:T(8,128)} %param.6) | copy-start | bytes 1540
  50.8 31.4 %copy-start.1 = (s32[8,128]{1,0:T(8,128)S(1)}, s32[8,128]{1,0:T(8,128)}, u32[]{:S(2)}) copy-start(s32[8,128]{1,0:T(8,128)} %get-tuple-element.7.first_ref) | copy-start | bytes 12292
  50.8 31.4 %copy-start.2 = (bf16[16,8]{0,1:T(8,128)(2,1)S(1)}, bf16[16,8]{0,1:T(8,128)(2,1)}, u32[]{:S(2)}) copy-start(bf16[16,8]{0,1:T(8,128)(2,1)} %param.7) | copy-start | bytes 772

commit v4 on v3

--- a/solution.py
+++ b/solution.py
@@ -8,28 +8,40 @@
 LANES = 128
 F32 = jnp.float32
 BF16 = jnp.bfloat16
-
-
-PACK_STEPS = 8
+UP_TILE = 256
+HEAD = 2
+DOWN_TILE = 512
+DOWN_GROUP = 4
+IN_FLIGHT = 6
+PIECE = 512
+
+
+def up_start(n, hidden):
+    return n % 2 * hidden + n // 2 * UP_TILE
 
 
 def pack_kernel(
-    route_ref, tokens_ref, out_ref, first_ref, route, tokens, blocks, first, low, high, source, in_sem, out_sem
+    route_ref, tokens_ref, gate_up_ref, out_ref, first_ref, head_ref, route, tokens, low, high, source, sem, head_sem
 ):
     top_count, row_count = route.shape
     chunks = tokens.shape[1] // LANES
     pitch = 2 * chunks
-    peers = blocks.shape[0] // pitch
-    step_peers = peers // PACK_STEPS
-
-    fetch_route = pltpu.make_async_copy(route_ref, route, in_sem.at[0])
-    fetch_tokens = pltpu.make_async_copy(tokens_ref, tokens, in_sem.at[1])
+    peers = out_ref.shape[0] // pitch
+    hidden = gate_up_ref.shape[2] // 2
+
+    fetch_route = pltpu.make_async_copy(route_ref, route, sem.at[2])
     fetch_route.start()
-    fetch_tokens.start()
+    fetch = pltpu.make_async_copy(tokens_ref, tokens, sem.at[0])
+    fetch.start()
+    heads = []
+    for n in range(HEAD):
+        tile = gate_up_ref.at[0, :, pl.ds(up_start(n, hidden), UP_TILE)]
+        heads.append(pltpu.make_async_copy(tile, head_ref.at[n], head_sem.at[n]))
+        heads[n].start()
+
     low[...] = jnp.zeros_like(low)
     high[...] = jnp.zeros_like(high)
     fetch_route.wait()
-
     peer = lax.broadcasted_iota(jnp.int32, (top_count, peers), 1)
     lowest = jnp.full((top_count, peers), row_count, jnp.int32)
     highest = jnp.full((top_count, peers), -1, jnp.int32)
@@ -41,12 +53,10 @@
     highest = jnp.max(highest, axis=0, keepdims=True)
     second = jnp.where(highest > lowest, highest, row_count)
     side = lax.broadcasted_iota(jnp.int32, (8, peers), 0)
-    first[...] = jnp.where(side == 0, lowest, second)
-    publish = pltpu.make_async_copy(first, source, in_sem.at[2])
+    first_ref[...] = jnp.where(side == 0, lowest, second)
+    publish = pltpu.make_async_copy(first_ref, source, sem.at[1])
     publish.start()
-    keep = pltpu.make_async_copy(first, first_ref, in_sem.at[3])
-    keep.start()
-    fetch_tokens.wait()
+    fetch.wait()
     for c in range(chunks):
         part = tokens[:, c * LANES : (c + 1) * LANES].astype(F32)
         low[pl.ds(2 * c, row_count, stride=pitch), :] = part
@@ -59,58 +69,45 @@
             a = pl.multiple_of(source[0, p] * pitch, 8)
             b = pl.multiple_of(source[1, p] * pitch, 8)
             pair.append(low[pl.ds(a, pitch), :] + high[pl.ds(b, pitch), :])
-        blocks[pl.ds(pl.multiple_of(i * 2 * pitch, 16), 2 * pitch), :] = jnp.concatenate(
+        out_ref[pl.ds(pl.multiple_of(i * 2 * pitch, 16), 2 * pitch), :] = jnp.concatenate(
             pair, axis=0
         ).astype(BF16)
         return 0
 
-    sends = []
-    for step in range(PACK_STEPS):
-        lax.fori_loop(step * step_peers // 2, (step + 1) * step_peers // 2, fill, 0, unroll=4)
-        span = pl.ds(step * step_peers * pitch, step_peers * pitch)
-        sends.append(pltpu.make_async_copy(blocks.at[span], out_ref.at[span], out_sem.at[step]))
-        sends[step].start()
-    keep.wait()
-    for send in sends:
-        send.wait()
-
-
-def pack(route, tokens, peers):
+    lax.fori_loop(0, peers // 2, fill, 0, unroll=4)
+    for copy in heads:
+        copy.wait()
+
+
+def pack(route, tokens, gate_up, peers):
     row_count, width = tokens.shape
     pitch = 2 * width // LANES
+    vmem = pl.BlockSpec(memory_space=pltpu.VMEM)
     anywhere = pl.BlockSpec(memory_space=pl.ANY)
     return pl.pallas_call(
         pack_kernel,
         out_shape=(
             jax.ShapeDtypeStruct((peers * pitch, LANES), BF16),
             jax.ShapeDtypeStruct((8, peers), jnp.int32),
+            jax.ShapeDtypeStruct((HEAD, width, UP_TILE), BF16),
         ),
-        in_specs=[anywhere, anywhere],
-        out_specs=(anywhere, anywhere),
+        in_specs=[anywhere, anywhere, anywhere],
+        out_specs=(vmem, vmem, vmem),
         scratch_shapes=[
             pltpu.VMEM(route.shape, jnp.int32),
             pltpu.VMEM(tokens.shape, BF16),
-            pltpu.VMEM((peers * pitch, LANES), BF16),
-            pltpu.VMEM((8, peers), jnp.int32),
             pltpu.VMEM(((row_count + 1) * pitch, LANES), F32),
             pltpu.VMEM(((row_count + 1) * pitch, LANES), F32),
             pltpu.SMEM((8, peers), jnp.int32),
-            pltpu.SemaphoreType.DMA((4,)),
-            pltpu.SemaphoreType.DMA((PACK_STEPS,)),
+            pltpu.SemaphoreType.DMA((3,)),
+            pltpu.SemaphoreType.DMA((HEAD,)),
         ],
-        compiler_params=pltpu.CompilerParams(vmem_limit_bytes=60000000),
+        compiler_params=pltpu.CompilerParams(vmem_limit_bytes=16 * 2**20),
         name="pack",
-    )(route, tokens)
-
-
-UP_TILE = 256
-DOWN_TILE = 512
-DOWN_GROUP = 4
-IN_FLIGHT = 6
-PIECE = 512
-
-
-def ffn_kernel(got_ref, gate_up_ref, down_ref, out_ref, wide, rows, gate_up, down, active, up_sem, down_sem):
+    )(route, tokens, gate_up)
+
+
+def ffn_kernel(got_ref, head_ref, gate_up_ref, down_ref, out_ref, wide, rows, gate_up, down, active, up_sem, down_sem):
     width = rows.shape[1]
     hidden = active.shape[1]
     chunks = width // LANES
@@ -120,13 +117,9 @@
     down_steps = width // DOWN_TILE
 
     copies = []
-    for n in range(2 * up_steps):
-        start = n % 2 * hidden + n // 2 * UP_TILE
-        copies.append(
-            pltpu.make_async_copy(
-                gate_up_ref.at[0, :, pl.ds(start, UP_TILE)], gate_up.at[n], up_sem.at[n]
-            )
-        )
+    for n in range(HEAD, 2 * up_steps):
+        tile = gate_up_ref.at[0, :, pl.ds(up_start(n, hidden), UP_TILE)]
+        copies.append(pltpu.make_async_copy(tile, gate_up.at[n - HEAD], up_sem.at[n - HEAD]))
     for n in range(down_steps):
         copies.append(
             pltpu.make_async_copy(
@@ -154,16 +147,19 @@
             ].astype(BF16)
 
     for step in range(up_steps):
-        take(2 * step)
-        take(2 * step + 1)
-        gate = jnp.dot(rows[...], gate_up[2 * step], preferred_element_type=F32)
-        up = jnp.dot(rows[...], gate_up[2 * step + 1], preferred_element_type=F32)
+        tiles = []
+        for n in (2 * step, 2 * step + 1):
+            if n >= HEAD:
+                take(n - HEAD)
+            tiles.append(head_ref.at[n] if n < HEAD else gate_up.at[n - HEAD])
+        gate = jnp.dot(rows[...], tiles[0][...], preferred_element_type=F32)
+        up = jnp.dot(rows[...], tiles[1][...], preferred_element_type=F32)
         active[:, step * UP_TILE : (step + 1) * UP_TILE] = (gate / (1 + jnp.exp(-gate)) * up).astype(BF16)
 
     for first in range(0, down_steps, DOWN_GROUP):
         steps = range(first, min(first + DOWN_GROUP, down_steps))
         for step in steps:
-            take(2 * up_steps + step)
+            take(2 * up_steps - HEAD + step)
         for step in steps:
             result = jnp.dot(active[...], down[step], preferred_element_type=F32)
             for q in range(DOWN_TILE // LANES):
@@ -181,17 +177,18 @@
     lax.fori_loop(0, peers * pitch // PIECE, narrow, 0)
 
 
-def expert_ffn(got, gate_up, down):
+def expert_ffn(got, head, gate_up, down):
     _, width, both = gate_up.shape
     hidden = both // 2
     total = got.shape[0]
     slots = total * LANES // width
-    up_tiles = both // UP_TILE
+    up_tiles = both // UP_TILE - HEAD
     down_tiles = width // DOWN_TILE
     return pl.pallas_call(
         ffn_kernel,
         out_shape=jax.ShapeDtypeStruct(got.shape, BF16),
         in_specs=[
+            pl.BlockSpec(memory_space=pltpu.VMEM),
             pl.BlockSpec(memory_space=pltpu.VMEM),
             pl.BlockSpec(memory_space=pl.ANY),
             pl.BlockSpec(memory_space=pl.ANY),
@@ -211,7 +208,7 @@
             flops=2 * slots * width * hidden * 3, bytes_accessed=6 * width * hidden, transcendentals=slots * hidden
         ),
         name="expert_ffn",
-    )(got, gate_up, down)
+    )(got, head, gate_up, down)
 
 
 def combine_kernel(
@@ -289,6 +286,10 @@
     )(route, first, weight, got)
 
 
+def stay_in_hbm(array):
+    return pltpu.with_memory_space_constraint(array, pltpu.HBM)
+
+
 def exchange(blocks, peers):
     shape = blocks.shape
     blocks = blocks.reshape(peers, -1, LANES)
@@ -299,9 +300,14 @@
     width = tokens.shape[1]
     peers = lax.axis_size("node") * lax.axis_size("local")
     route = route.T
-    send, first = pack(route, tokens, peers)
+    send, first, head = pack(
+        stay_in_hbm(route),
+        stay_in_hbm(tokens),
+        stay_in_hbm(gate_up),
+        peers,
+    )
     got = exchange(send, peers)
-    result = expert_ffn(got, gate_up, down)
+    result = expert_ffn(got, head, stay_in_hbm(gate_up), stay_in_hbm(down))
     back = exchange(result, peers)
     return combine(route, first, combine_weight.T, back, width)
 

time: 84.3 us -> 82.3 us (0.976)
  Pallas kernels: 14.4 us -> 12.8 us
    pallas_call x1, Pallas kernels: 9.54 us -> 8.48 us  [expert_ffn(): pl.pallas_call(ffn_kernel, out_shape=jax.ShapeDtypeStruct(got.shape, BF16...]
where the time goes in v4:
time: 82.3 us; the launch traced here: 82.2 us
  blocking collectives  69.4 us (84%)
  Pallas kernels  12.8 us (16%)
    all_to_all x2, blocking collectives, exchange(): lax.all_to_all(blocks, ('node', 'local'), split_axis=0, concat_axis=0, ti...  69.4 us
    pallas_call x1, Pallas kernels, expert_ffn(): pl.pallas_call(ffn_kernel, out_shape=jax.ShapeDtypeStruct(got.shape, BF16...  8.48 us
    pallas_call x1, Pallas kernels, pack(): pl.pallas_call(pack_kernel, out_shape=(jax.ShapeDtypeStruct((peers * pitc...  2.38 us
    pallas_call x1, Pallas kernels, combine(): pl.pallas_call(combine_kernel, out_shape=jax.ShapeDtypeStruct((row_count,...  1.89 us

profile of v4, /device:TPU:0, one launch (start us, length us, event | category | flops | bytes accessed | tf_op | source)
XLA Modules:
  0.0 82.2 jit_solution(15671084691712144640)
XLA Ops:
  0.0 2.4 %pack.1 = (bf16[7168,128]{1,0:T(8,128)(2,1)S(1)}, s32[8,128]{1,0:T(8,128)S(1)}, bf16[2,3584,256]{2,1,0:T(8,128)(2,1)S(1)}) custom-call(s32[8,16]{1,0:T(8,128)} %bitcast.10, bf16[16,3584]{1,0:T(8,128)(2,1)} %tokens_ref.1, bf16[1,3584,2048]{2,1,0:T(8,128)(2,1)} %gate_up_ref.3), custom_call_target="tpu_custom_call" | custom-call | tf_op jit(solution)/shard_map/pack/pallas_call | solution.py:87
  2.4 38.0 %all_to_all.10 = bf16[128,56,128]{2,1,0:T(8,128)(2,1)S(1)} all-to-all(bf16[128,56,128]{2,1,0:T(8,128)(2,1)S(1)} %bitcast.9), channel_id=1, replica_groups=mesh['node'=8,'local'=16] {'node','local'}, dimensions={0} | all-to-all | bytes 3670016 | tf_op jit(solution)/shard_map/all_to_all | solution.py:296
  40.4 8.5 %expert_ffn.1 = bf16[7168,128]{1,0:T(8,128)(2,1)S(1)} custom-call(bf16[7168,128]{1,0:T(8,128)(2,1)S(1)} %bitcast.6, bf16[2,3584,256]{2,1,0:T(8,128)(2,1)S(1)} %get-tuple-element.10.head_ref, bf16[1,3584,2048]{2,1,0:T(8,128)(2,1)} %gate_up_ref.3, bf16[1,1024,3584]{2,1,0:T(8,128)(2,1)} %down_ref.1), custom_call_target="tpu_custom_call" | custom-call | flops 5637144576 | bytes 22020096 | tf_op jit(solution)/shard_map/expert_ffn/pallas_call | solution.py:187
  48.9 0.0 copy-start
  48.9 0.0 copy-start.1
  48.9 31.3 %all_to_all.11 = bf16[128,56,128]{2,1,0:T(8,128)(2,1)S(1)} all-to-all(bf16[128,56,128]{2,1,0:T(8,128)(2,1)S(1)} %bitcast.7), channel_id=1, replica_groups=mesh['node'=8,'local'=16] {'node','local'}, dimensions={0} | all-to-all | bytes 3670016 | tf_op jit(solution)/shard_map/all_to_all | solution.py:296
  80.3 0.0 copy-done
  80.3 0.0 copy-done.1
  80.3 1.9 %combine.1 = bf16[16,3584]{1,0:T(8,128)(2,1)} custom-call(s32[8,16]{1,0:T(8,128)S(1)} %bitcast.11, s32[8,128]{1,0:T(8,128)S(1)} %get-tuple-element.8.first_ref, bf16[8,16]{1,0:T(8,128)(2,1)S(1)} %bitcast.12, bf16[7168,128]{1,0:T(8,128)(2,1)S(1)} %bitcast.8), custom_call_target="tpu_custom_call" | custom-call | tf_op jit(solution)/shard_map/combine/pallas_call | solution.py:269
Async XLA Ops:
  48.9 31.4 %copy-start = (s32[16,8]{0,1:T(8,128)S(1)}, s32[16,8]{0,1:T(8,128)}, u32[]{:S(2)}) copy-start(s32[16,8]{0,1:T(8,128)} %param.6) | copy-start | bytes 1540
  48.9 31.4 %copy-start.1 = (bf16[16,8]{0,1:T(8,128)(2,1)S(1)}, bf16[16,8]{0,1:T(8,128)(2,1)}, u32[]{:S(2)}) copy-start(bf16[16,8]{0,1:T(8,128)(2,1)} %param.7) | copy-start | bytes 772

commit v5 on v4

--- a/solution.py
+++ b/solution.py
@@ -11,8 +11,6 @@
 UP_TILE = 256
 HEAD = 2
 DOWN_TILE = 512
-DOWN_GROUP = 4
-IN_FLIGHT = 6
 PIECE = 512
 
 
@@ -107,32 +105,23 @@
     )(route, tokens, gate_up)
 
 
-def ffn_kernel(got_ref, head_ref, gate_up_ref, down_ref, out_ref, wide, rows, gate_up, down, active, up_sem, down_sem):
+def ffn_kernel(got_ref, head_ref, gate_up_ref, down_ref, out_ref, wide, rows, gate_up, active, up_sem):
     width = rows.shape[1]
     hidden = active.shape[1]
     chunks = width // LANES
     pitch = 2 * chunks
     peers = got_ref.shape[0] // pitch
     up_steps = hidden // UP_TILE
-    down_steps = width // DOWN_TILE
 
     copies = []
     for n in range(HEAD, 2 * up_steps):
         tile = gate_up_ref.at[0, :, pl.ds(up_start(n, hidden), UP_TILE)]
         copies.append(pltpu.make_async_copy(tile, gate_up.at[n - HEAD], up_sem.at[n - HEAD]))
-    for n in range(down_steps):
-        copies.append(
-            pltpu.make_async_copy(
-                down_ref.at[0, :, pl.ds(n * DOWN_TILE, DOWN_TILE)], down.at[n], down_sem.at[n]
-            )
-        )
-    for copy in copies[:IN_FLIGHT]:
+    for copy in copies[:2]:
         copy.start()
 
-    def take(n):
-        copies[n].wait()
-        if n + IN_FLIGHT < len(copies):
-            copies[n + IN_FLIGHT].start()
+    for copy in copies[2:]:
+        copy.start(priority=1)
 
     def widen(i, _):
         span = pl.ds(pl.multiple_of(i * PIECE, PIECE), PIECE)
@@ -150,24 +139,19 @@
         tiles = []
         for n in (2 * step, 2 * step + 1):
             if n >= HEAD:
-                take(n - HEAD)
+                copies[n - HEAD].wait()
             tiles.append(head_ref.at[n] if n < HEAD else gate_up.at[n - HEAD])
         gate = jnp.dot(rows[...], tiles[0][...], preferred_element_type=F32)
         up = jnp.dot(rows[...], tiles[1][...], preferred_element_type=F32)
         active[:, step * UP_TILE : (step + 1) * UP_TILE] = (gate / (1 + jnp.exp(-gate)) * up).astype(BF16)
 
-    for first in range(0, down_steps, DOWN_GROUP):
-        steps = range(first, min(first + DOWN_GROUP, down_steps))
-        for step in steps:
-            take(2 * up_steps - HEAD + step)
-        for step in steps:
-            result = jnp.dot(active[...], down[step], preferred_element_type=F32)
-            for q in range(DOWN_TILE // LANES):
-                c = step * (DOWN_TILE // LANES) + q
-                for r in range(2):
-                    wide[pl.ds(2 * c + r, peers, stride=pitch), :] = result[
-                        r * peers : (r + 1) * peers, q * LANES : (q + 1) * LANES
-                    ]
+    for n in range(0, width, DOWN_TILE):
+        result = jnp.dot(active[...], down_ref[0, :, n : n + DOWN_TILE], preferred_element_type=F32)
+        for q in range(0, DOWN_TILE, LANES):
+            for r in range(2):
+                wide[pl.ds(2 * (n + q) // LANES + r, peers, stride=pitch), :] = result[
+                    r * peers : (r + 1) * peers, q : q + LANES
+                ]
 
     def narrow(i, _):
         span = pl.ds(pl.multiple_of(i * PIECE, PIECE), PIECE)
@@ -183,27 +167,20 @@
     total = got.shape[0]
     slots = total * LANES // width
     up_tiles = both // UP_TILE - HEAD
-    down_tiles = width // DOWN_TILE
+    vmem = pl.BlockSpec(memory_space=pltpu.VMEM)
     return pl.pallas_call(
         ffn_kernel,
         out_shape=jax.ShapeDtypeStruct(got.shape, BF16),
-        in_specs=[
-            pl.BlockSpec(memory_space=pltpu.VMEM),
-            pl.BlockSpec(memory_space=pltpu.VMEM),
-            pl.BlockSpec(memory_space=pl.ANY),
-            pl.BlockSpec(memory_space=pl.ANY),
-        ],
-        out_specs=pl.BlockSpec(memory_space=pltpu.VMEM),
+        in_specs=[vmem, vmem, pl.BlockSpec(memory_space=pl.ANY), vmem],
+        out_specs=vmem,
         scratch_shapes=[
             pltpu.VMEM((total, LANES), F32),
             pltpu.VMEM((slots, width), BF16),
             pltpu.VMEM((up_tiles, width, UP_TILE), BF16),
-            pltpu.VMEM((down_tiles, hidden, DOWN_TILE), BF16),
             pltpu.VMEM((slots, hidden), BF16),
             pltpu.SemaphoreType.DMA((up_tiles,)),
-            pltpu.SemaphoreType.DMA((down_tiles,)),
         ],
-        compiler_params=pltpu.CompilerParams(vmem_limit_bytes=44 * 2**20),
+        compiler_params=pltpu.CompilerParams(vmem_limit_bytes=30 * 2**20),
         cost_estimate=pl.CostEstimate(
             flops=2 * slots * width * hidden * 3, bytes_accessed=6 * width * hidden, transcendentals=slots * hidden
         ),
@@ -307,7 +284,7 @@
         peers,
     )
     got = exchange(send, peers)
-    result = expert_ffn(got, head, stay_in_hbm(gate_up), stay_in_hbm(down))
+    result = expert_ffn(got, head, stay_in_hbm(gate_up), down)
     back = exchange(result, peers)
     return combine(route, first, combine_weight.T, back, width)
 

time: 82.3 us -> 81.9 us (level)
  no operation moved by 1% of the time
where the time goes in v5:
time: 81.9 us; the launch traced here: 81.7 us
  blocking collectives  69.4 us (85%)
  Pallas kernels  12.3 us (15%)
    all_to_all x2, blocking collectives, exchange(): lax.all_to_all(blocks, ('node', 'local'), split_axis=0, concat_axis=0, ti...  69.4 us
    pallas_call x1, Pallas kernels, expert_ffn(): pl.pallas_call(ffn_kernel, out_shape=jax.ShapeDtypeStruct(got.shape, BF16...  7.89 us
    pallas_call x1, Pallas kernels, pack(): pl.pallas_call(pack_kernel, out_shape=(jax.ShapeDtypeStruct((peers * pitc...  2.53 us
    pallas_call x1, Pallas kernels, combine(): pl.pallas_call(combine_kernel, out_shape=jax.ShapeDtypeStruct((row_count,...  1.89 us

profile of v5, /device:TPU:0, one launch (start us, length us, event | category | flops | bytes accessed | tf_op | source)
XLA Modules:
  0.0 81.7 jit_solution(6770350956440579982)
XLA Ops:
  0.0 0.0 copy-start
  0.0 2.5 %pack.1 = (bf16[7168,128]{1,0:T(8,128)(2,1)S(1)}, s32[8,128]{1,0:T(8,128)S(1)}, bf16[2,3584,256]{2,1,0:T(8,128)(2,1)S(1)}) custom-call(s32[8,16]{1,0:T(8,128)} %bitcast.10, bf16[16,3584]{1,0:T(8,128)(2,1)} %tokens_ref.1, bf16[1,3584,2048]{2,1,0:T(8,128)(2,1)} %gate_up_ref.3), custom_call_target="tpu_custom_call" | custom-call | tf_op jit(solution)/shard_map/pack/pallas_call | solution.py:85
  2.5 38.0 %all_to_all.10 = bf16[128,56,128]{2,1,0:T(8,128)(2,1)S(1)} all-to-all(bf16[128,56,128]{2,1,0:T(8,128)(2,1)S(1)} %bitcast.9), channel_id=1, replica_groups=mesh['node'=8,'local'=16] {'node','local'}, dimensions={0} | all-to-all | bytes 3670016 | tf_op jit(solution)/shard_map/all_to_all | solution.py:273
  40.6 0.0 copy-done
  40.6 7.9 %expert_ffn.1 = bf16[7168,128]{1,0:T(8,128)(2,1)S(1)} custom-call(bf16[7168,128]{1,0:T(8,128)(2,1)S(1)} %bitcast.6, bf16[2,3584,256]{2,1,0:T(8,128)(2,1)S(1)} %get-tuple-element.10.head_ref, bf16[1,3584,2048]{2,1,0:T(8,128)(2,1)} %gate_up_ref.3, bf16[1,1024,3584]{2,1,0:T(8,128)(2,1)S(1)} %copy-done), custom_call_target="tpu_custom_call" | custom-call | flops 5637144576 | bytes 22020096 | tf_op jit(solution)/shard_map/expert_ffn/pallas_call | solution.py:171
  48.5 0.0 copy-start.1
  48.5 0.0 copy-start.2
  48.5 31.3 %all_to_all.11 = bf16[128,56,128]{2,1,0:T(8,128)(2,1)S(1)} all-to-all(bf16[128,56,128]{2,1,0:T(8,128)(2,1)S(1)} %bitcast.7), channel_id=1, replica_groups=mesh['node'=8,'local'=16] {'node','local'}, dimensions={0} | all-to-all | bytes 3670016 | tf_op jit(solution)/shard_map/all_to_all | solution.py:273
  79.8 0.0 copy-done.1
  79.8 0.0 copy-done.2
  79.8 1.9 %combine.1 = bf16[16,3584]{1,0:T(8,128)(2,1)} custom-call(s32[8,16]{1,0:T(8,128)S(1)} %bitcast.11, s32[8,128]{1,0:T(8,128)S(1)} %get-tuple-element.8.first_ref, bf16[8,16]{1,0:T(8,128)(2,1)S(1)} %bitcast.12, bf16[7168,128]{1,0:T(8,128)(2,1)S(1)} %bitcast.8), custom_call_target="tpu_custom_call" | custom-call | tf_op jit(solution)/shard_map/combine/pallas_call | solution.py:246
Async XLA Ops:
  0.0 40.6 %copy-start = (bf16[1,1024,3584]{2,1,0:T(8,128)(2,1)S(1)}, bf16[1,1024,3584]{2,1,0:T(8,128)(2,1)}, u32[]{:S(2)}) copy-start(bf16[1,1024,3584]{2,1,0:T(8,128)(2,1)} %down_ref.1) | copy-start | bytes 22020100
  48.5 31.4 %copy-start.1 = (s32[16,8]{0,1:T(8,128)S(1)}, s32[16,8]{0,1:T(8,128)}, u32[]{:S(2)}) copy-start(s32[16,8]{0,1:T(8,128)} %param.6) | copy-start | bytes 1540
  48.5 31.4 %copy-start.2 = (bf16[16,8]{0,1:T(8,128)(2,1)S(1)}, bf16[16,8]{0,1:T(8,128)(2,1)}, u32[]{:S(2)}) copy-start(bf16[16,8]{0,1:T(8,128)(2,1)} %param.7) | copy-start | bytes 772

commit v6 on v5

--- a/solution.py
+++ b/solution.py
@@ -9,34 +9,22 @@
 F32 = jnp.float32
 BF16 = jnp.bfloat16
 UP_TILE = 256
-HEAD = 2
 DOWN_TILE = 512
 PIECE = 512
 
 
-def up_start(n, hidden):
-    return n % 2 * hidden + n // 2 * UP_TILE
-
-
 def pack_kernel(
-    route_ref, tokens_ref, gate_up_ref, out_ref, first_ref, head_ref, route, tokens, low, high, source, sem, head_sem
+    route_ref, tokens_ref, out_ref, first_ref, route, tokens, low, high, source, sem
 ):
     top_count, row_count = route.shape
     chunks = tokens.shape[1] // LANES
     pitch = 2 * chunks
     peers = out_ref.shape[0] // pitch
-    hidden = gate_up_ref.shape[2] // 2
 
     fetch_route = pltpu.make_async_copy(route_ref, route, sem.at[2])
     fetch_route.start()
     fetch = pltpu.make_async_copy(tokens_ref, tokens, sem.at[0])
     fetch.start()
-    heads = []
-    for n in range(HEAD):
-        tile = gate_up_ref.at[0, :, pl.ds(up_start(n, hidden), UP_TILE)]
-        heads.append(pltpu.make_async_copy(tile, head_ref.at[n], head_sem.at[n]))
-        heads[n].start()
-
     low[...] = jnp.zeros_like(low)
     high[...] = jnp.zeros_like(high)
     fetch_route.wait()
@@ -73,11 +61,9 @@
         return 0
 
     lax.fori_loop(0, peers // 2, fill, 0, unroll=4)
-    for copy in heads:
-        copy.wait()
-
-
-def pack(route, tokens, gate_up, peers):
+
+
+def pack(route, tokens, peers):
     row_count, width = tokens.shape
     pitch = 2 * width // LANES
     vmem = pl.BlockSpec(memory_space=pltpu.VMEM)
@@ -87,10 +73,9 @@
         out_shape=(
             jax.ShapeDtypeStruct((peers * pitch, LANES), BF16),
             jax.ShapeDtypeStruct((8, peers), jnp.int32),
-            jax.ShapeDtypeStruct((HEAD, width, UP_TILE), BF16),
         ),
-        in_specs=[anywhere, anywhere, anywhere],
-        out_specs=(vmem, vmem, vmem),
+        in_specs=[anywhere, anywhere],
+        out_specs=(vmem, vmem),
         scratch_shapes=[
             pltpu.VMEM(route.shape, jnp.int32),
             pltpu.VMEM(tokens.shape, BF16),
@@ -98,30 +83,19 @@
             pltpu.VMEM(((row_count + 1) * pitch, LANES), F32),
             pltpu.SMEM((8, peers), jnp.int32),
             pltpu.SemaphoreType.DMA((3,)),
-            pltpu.SemaphoreType.DMA((HEAD,)),
         ],
         compiler_params=pltpu.CompilerParams(vmem_limit_bytes=16 * 2**20),
+        cost_estimate=pl.CostEstimate(flops=20000000000, bytes_accessed=1000, transcendentals=0),
         name="pack",
-    )(route, tokens, gate_up)
-
-
-def ffn_kernel(got_ref, head_ref, gate_up_ref, down_ref, out_ref, wide, rows, gate_up, active, up_sem):
+    )(route, tokens)
+
+
+def ffn_kernel(got_ref, gate_up_ref, down_ref, out_ref, wide, rows, active):
     width = rows.shape[1]
     hidden = active.shape[1]
     chunks = width // LANES
     pitch = 2 * chunks
     peers = got_ref.shape[0] // pitch
-    up_steps = hidden // UP_TILE
-
-    copies = []
-    for n in range(HEAD, 2 * up_steps):
-        tile = gate_up_ref.at[0, :, pl.ds(up_start(n, hidden), UP_TILE)]
-        copies.append(pltpu.make_async_copy(tile, gate_up.at[n - HEAD], up_sem.at[n - HEAD]))
-    for copy in copies[:2]:
-        copy.start()
-
-    for copy in copies[2:]:
-        copy.start(priority=1)
 
     def widen(i, _):
         span = pl.ds(pl.multiple_of(i * PIECE, PIECE), PIECE)
@@ -135,15 +109,10 @@
                 pl.ds(2 * c + r, peers, stride=pitch), :
             ].astype(BF16)
 
-    for step in range(up_steps):
-        tiles = []
-        for n in (2 * step, 2 * step + 1):
-            if n >= HEAD:
-                copies[n - HEAD].wait()
-            tiles.append(head_ref.at[n] if n < HEAD else gate_up.at[n - HEAD])
-        gate = jnp.dot(rows[...], tiles[0][...], preferred_element_type=F32)
-        up = jnp.dot(rows[...], tiles[1][...], preferred_element_type=F32)
-        active[:, step * UP_TILE : (step + 1) * UP_TILE] = (gate / (1 + jnp.exp(-gate)) * up).astype(BF16)
+    for n in range(0, hidden, UP_TILE):
+        gate = jnp.dot(rows[...], gate_up_ref[0, :, n : n + UP_TILE], preferred_element_type=F32)
+        up = jnp.dot(rows[...], gate_up_ref[0, :, hidden + n : hidden + n + UP_TILE], preferred_element_type=F32)
+        active[:, n : n + UP_TILE] = (gate / (1 + jnp.exp(-gate)) * up).astype(BF16)
 
     for n in range(0, width, DOWN_TILE):
         result = jnp.dot(active[...], down_ref[0, :, n : n + DOWN_TILE], preferred_element_type=F32)
@@ -161,31 +130,27 @@
     lax.fori_loop(0, peers * pitch // PIECE, narrow, 0)
 
 
-def expert_ffn(got, head, gate_up, down):
+def expert_ffn(got, gate_up, down):
     _, width, both = gate_up.shape
     hidden = both // 2
     total = got.shape[0]
     slots = total * LANES // width
-    up_tiles = both // UP_TILE - HEAD
-    vmem = pl.BlockSpec(memory_space=pltpu.VMEM)
     return pl.pallas_call(
         ffn_kernel,
         out_shape=jax.ShapeDtypeStruct(got.shape, BF16),
-        in_specs=[vmem, vmem, pl.BlockSpec(memory_space=pl.ANY), vmem],
-        out_specs=vmem,
+        in_specs=[pl.BlockSpec(memory_space=pltpu.VMEM)] * 3,
+        out_specs=pl.BlockSpec(memory_space=pltpu.VMEM),
         scratch_shapes=[
             pltpu.VMEM((total, LANES), F32),
             pltpu.VMEM((slots, width), BF16),
-            pltpu.VMEM((up_tiles, width, UP_TILE), BF16),
             pltpu.VMEM((slots, hidden), BF16),
-            pltpu.SemaphoreType.DMA((up_tiles,)),
         ],
-        compiler_params=pltpu.CompilerParams(vmem_limit_bytes=30 * 2**20),
+        compiler_params=pltpu.CompilerParams(vmem_limit_bytes=12 * 2**20),
         cost_estimate=pl.CostEstimate(
             flops=2 * slots * width * hidden * 3, bytes_accessed=6 * width * hidden, transcendentals=slots * hidden
         ),
         name="expert_ffn",
-    )(got, head, gate_up, down)
+    )(got, gate_up, down)
 
 
 def combine_kernel(
@@ -277,14 +242,9 @@
     width = tokens.shape[1]
     peers = lax.axis_size("node") * lax.axis_size("local")
     route = route.T
-    send, first, head = pack(
-        stay_in_hbm(route),
-        stay_in_hbm(tokens),
-        stay_in_hbm(gate_up),
-        peers,
-    )
+    send, first = pack(stay_in_hbm(route), stay_in_hbm(tokens), peers)
     got = exchange(send, peers)
-    result = expert_ffn(got, head, stay_in_hbm(gate_up), down)
+    result = expert_ffn(got, gate_up, down)
     back = exchange(result, peers)
     return combine(route, first, combine_weight.T, back, width)
 

time: 81.9 us -> 80.7 us (0.985)
  Pallas kernels: 12.3 us -> 11.1 us
    pallas_call x1, Pallas kernels: 7.89 us -> 6.87 us  [expert_ffn(): pl.pallas_call(ffn_kernel, out_shape=jax.ShapeDtypeStruct(got.shape, BF16...]
where the time goes in v6:
time: 80.7 us; the launch traced here: 80.5 us
  blocking collectives  69.4 us (86%)
  Pallas kernels  11.1 us (14%)
    all_to_all x2, blocking collectives, exchange(): lax.all_to_all(blocks, ('node', 'local'), split_axis=0, concat_axis=0, ti...  69.4 us
    pallas_call x1, Pallas kernels, expert_ffn(): pl.pallas_call(ffn_kernel, out_shape=jax.ShapeDtypeStruct(got.shape, BF16...  6.87 us
    pallas_call x1, Pallas kernels, pack(): pl.pallas_call(pack_kernel, out_shape=(jax.ShapeDtypeStruct((peers * pitc...  2.34 us
    pallas_call x1, Pallas kernels, combine(): pl.pallas_call(combine_kernel, out_shape=jax.ShapeDtypeStruct((row_count,...  1.89 us

profile of v6, /device:TPU:0, one launch (start us, length us, event | category | flops | bytes accessed | tf_op | source)
XLA Modules:
  0.0 80.5 jit_solution(7445949576297535042)
XLA Ops:
  0.0 0.0 copy-start
  0.0 0.0 copy-start.1
  0.0 2.3 %pack.1 = (bf16[7168,128]{1,0:T(8,128)(2,1)S(1)}, s32[8,128]{1,0:T(8,128)S(1)}) custom-call(s32[8,16]{1,0:T(8,128)} %bitcast.10, bf16[16,3584]{1,0:T(8,128)(2,1)} %tokens_ref.1), custom_call_target="tpu_custom_call" | custom-call | flops 20000000000 | bytes 1000 | tf_op jit(solution)/shard_map/pack/pallas_call | solution.py:71
  2.4 38.0 %all_to_all.10 = bf16[128,56,128]{2,1,0:T(8,128)(2,1)S(1)} all-to-all(bf16[128,56,128]{2,1,0:T(8,128)(2,1)S(1)} %bitcast.9), channel_id=1, replica_groups=mesh['node'=8,'local'=16] {'node','local'}, dimensions={0} | all-to-all | bytes 3670016 | tf_op jit(solution)/shard_map/all_to_all | solution.py:238
  40.4 0.0 copy-done
  40.4 0.0 copy-done.1
  40.4 6.9 %expert_ffn.1 = bf16[7168,128]{1,0:T(8,128)(2,1)S(1)} custom-call(bf16[7168,128]{1,0:T(8,128)(2,1)S(1)} %bitcast.6, bf16[1,3584,2048]{2,1,0:T(8,128)(2,1)S(1)} %copy-done, bf16[1,1024,3584]{2,1,0:T(8,128)(2,1)S(1)} %copy-done.1), custom_call_target="tpu_custom_call" | custom-call | flops 5637144576 | bytes 22020096 | tf_op jit(solution)/shard_map/expert_ffn/pallas_call | solution.py:138
  47.3 0.0 copy-start.2
  47.3 0.0 copy-start.3
  47.3 31.3 %all_to_all.11 = bf16[128,56,128]{2,1,0:T(8,128)(2,1)S(1)} all-to-all(bf16[128,56,128]{2,1,0:T(8,128)(2,1)S(1)} %bitcast.7), channel_id=1, replica_groups=mesh['node'=8,'local'=16] {'node','local'}, dimensions={0} | all-to-all | bytes 3670016 | tf_op jit(solution)/shard_map/all_to_all | solution.py:238
  78.6 0.0 copy-done.2
  78.6 0.0 copy-done.3
  78.6 1.9 %combine.1 = bf16[16,3584]{1,0:T(8,128)(2,1)} custom-call(s32[8,16]{1,0:T(8,128)S(1)} %bitcast.11, s32[8,128]{1,0:T(8,128)S(1)} %get-tuple-element.7.first_ref, bf16[8,16]{1,0:T(8,128)(2,1)S(1)} %bitcast.12, bf16[7168,128]{1,0:T(8,128)(2,1)S(1)} %bitcast.8), custom_call_target="tpu_custom_call" | custom-call | tf_op jit(solution)/shard_map/combine/pallas_call | solution.py:211
Async XLA Ops:
  0.0 40.4 %copy-start = (bf16[1,3584,2048]{2,1,0:T(8,128)(2,1)S(1)}, bf16[1,3584,2048]{2,1,0:T(8,128)(2,1)}, u32[]{:S(2)}) copy-start(bf16[1,3584,2048]{2,1,0:T(8,128)(2,1)} %gate_up_ref.1) | copy-start | bytes 44040196
  0.0 40.4 %copy-start.1 = (bf16[1,1024,3584]{2,1,0:T(8,128)(2,1)S(1)}, bf16[1,1024,3584]{2,1,0:T(8,128)(2,1)}, u32[]{:S(2)}) copy-start(bf16[1,1024,3584]{2,1,0:T(8,128)(2,1)} %down_ref.1) | copy-start | bytes 22020100
  47.3 31.4 %copy-start.2 = (s32[16,8]{0,1:T(8,128)S(1)}, s32[16,8]{0,1:T(8,128)}, u32[]{:S(2)}) copy-start(s32[16,8]{0,1:T(8,128)} %param.6) | copy-start | bytes 1540
  47.3 31.4 %copy-start.3 = (bf16[16,8]{0,1:T(8,128)(2,1)S(1)}, bf16[16,8]{0,1:T(8,128)(2,1)}, u32[]{:S(2)}) copy-start(bf16[16,8]{0,1:T(8,128)(2,1)} %param.7) | copy-start | bytes 772

commit v7 on v6

--- a/solution.py
+++ b/solution.py
@@ -8,7 +8,8 @@
 LANES = 128
 F32 = jnp.float32
 BF16 = jnp.bfloat16
-UP_TILE = 256
+UP_TILE = 512
+DEPTH_TILE = 512
 DOWN_TILE = 512
 PIECE = 512
 
@@ -85,7 +86,7 @@
             pltpu.SemaphoreType.DMA((3,)),
         ],
         compiler_params=pltpu.CompilerParams(vmem_limit_bytes=16 * 2**20),
-        cost_estimate=pl.CostEstimate(flops=20000000000, bytes_accessed=1000, transcendentals=0),
+        cost_estimate=pl.CostEstimate(flops=20_000_000_000, bytes_accessed=1000, transcendentals=0),
         name="pack",
     )(route, tokens)
 
@@ -103,15 +104,26 @@
         return 0
 
     lax.fori_loop(0, peers * pitch // PIECE, widen, 0)
-    for c in range(chunks):
-        for r in range(2):
-            rows[r * peers : (r + 1) * peers, c * LANES : (c + 1) * LANES] = wide[
-                pl.ds(2 * c + r, peers, stride=pitch), :
-            ].astype(BF16)
+    def build(depth):
+        for c in range(depth // LANES, (depth + DEPTH_TILE) // LANES):
+            for r in range(2):
+                rows[r * peers : (r + 1) * peers, c * LANES : (c + 1) * LANES] = wide[
+                    pl.ds(2 * c + r, peers, stride=pitch), :
+                ].astype(BF16)
 
     for n in range(0, hidden, UP_TILE):
-        gate = jnp.dot(rows[...], gate_up_ref[0, :, n : n + UP_TILE], preferred_element_type=F32)
-        up = jnp.dot(rows[...], gate_up_ref[0, :, hidden + n : hidden + n + UP_TILE], preferred_element_type=F32)
+        if n == 0:
+            gate = up = 0
+            for depth in range(0, width, DEPTH_TILE):
+                build(depth)
+                span = slice(depth, depth + DEPTH_TILE)
+                gate += jnp.dot(rows[:, span], gate_up_ref[0, span, :UP_TILE], preferred_element_type=F32)
+                up += jnp.dot(
+                    rows[:, span], gate_up_ref[0, span, hidden : hidden + UP_TILE], preferred_element_type=F32
+                )
+        else:
+            gate = jnp.dot(rows[...], gate_up_ref[0, :, n : n + UP_TILE], preferred_element_type=F32)
+            up = jnp.dot(rows[...], gate_up_ref[0, :, hidden + n : hidden + n + UP_TILE], preferred_element_type=F32)
         active[:, n : n + UP_TILE] = (gate / (1 + jnp.exp(-gate)) * up).astype(BF16)
 
     for n in range(0, width, DOWN_TILE):
@@ -154,32 +166,27 @@
 
 
 def combine_kernel(
-    route_ref, first_ref, weight_ref, got_ref, out_ref, wide, total, narrow, scale, route, first, weight, sem
+    route_ref, first_ref, weight_ref, got_ref, out_ref, wide, total, scale, route, first, weight, sem
 ):
     top_count, row_count = route.shape
     chunks = out_ref.shape[1] // LANES
     pitch = 2 * chunks
     peers = got_ref.shape[0] // pitch
 
-    fetch_weight = pltpu.make_async_copy(weight_ref, narrow, sem.at[0])
-    fetch_route = pltpu.make_async_copy(route_ref, route, sem.at[1])
-    fetch_first = pltpu.make_async_copy(first_ref, first, sem.at[2])
-    fetch_weight.start()
+    fetch_route = pltpu.make_async_copy(route_ref, route, sem.at[0])
+    fetch_first = pltpu.make_async_copy(first_ref, first, sem.at[1])
     fetch_route.start()
     fetch_first.start()
+    scale[...] = weight_ref[...].astype(F32)
+    publish = pltpu.make_async_copy(scale, weight, sem.at[2])
+    publish.start()
 
     def widen(i, _):
         span = pl.ds(pl.multiple_of(i * PIECE, PIECE), PIECE)
         wide[span, :] = got_ref[span, :].astype(F32)
         return 0
 
-    pieces = peers * pitch // PIECE
-    lax.fori_loop(0, pieces // 2, widen, 0)
-    fetch_weight.wait()
-    scale[...] = narrow[...].astype(F32)
-    publish = pltpu.make_async_copy(scale, weight, sem.at[3])
-    publish.start()
-    lax.fori_loop(pieces // 2, pieces, widen, 0)
+    lax.fori_loop(0, peers * pitch // PIECE, widen, 0)
     fetch_route.wait()
     fetch_first.wait()
     publish.wait()
@@ -211,17 +218,16 @@
     return pl.pallas_call(
         combine_kernel,
         out_shape=jax.ShapeDtypeStruct((row_count, width), BF16),
-        in_specs=[anywhere, anywhere, anywhere, vmem],
+        in_specs=[anywhere, anywhere, vmem, vmem],
         out_specs=vmem,
         scratch_shapes=[
             pltpu.VMEM(got.shape, F32),
             pltpu.VMEM((row_count * pitch, LANES), F32),
-            pltpu.VMEM(weight.shape, BF16),
             pltpu.VMEM(weight.shape, F32),
             pltpu.SMEM(route.shape, jnp.int32),
             pltpu.SMEM(first.shape, jnp.int32),
             pltpu.SMEM(weight.shape, F32),
-            pltpu.SemaphoreType.DMA((4,)),
+            pltpu.SemaphoreType.DMA((3,)),
         ],
         compiler_params=pltpu.CompilerParams(vmem_limit_bytes=24 * 2**20),
         name="combine",

time: 80.7 us -> 80.4 us (level)
  no operation moved by 1% of the time
where the time goes in v7:
time: 80.4 us; the launch traced here: 80.3 us
  blocking collectives  69.4 us (86%)
  Pallas kernels  10.9 us (14%)
    all_to_all x2, blocking collectives, exchange(): lax.all_to_all(blocks, ('node', 'local'), split_axis=0, concat_axis=0, ti...  69.4 us
    pallas_call x1, Pallas kernels, expert_ffn(): pl.pallas_call(ffn_kernel, out_shape=jax.ShapeDtypeStruct(got.shape, BF16...  6.69 us
    pallas_call x1, Pallas kernels, pack(): pl.pallas_call(pack_kernel, out_shape=(jax.ShapeDtypeStruct((peers * pitc...  2.34 us
    pallas_call x1, Pallas kernels, combine(): pl.pallas_call(combine_kernel, out_shape=jax.ShapeDtypeStruct((row_count,...  1.87 us

profile of v7, /device:TPU:0, one launch (start us, length us, event | category | flops | bytes accessed | tf_op | source)
XLA Modules:
  0.0 80.3 jit_solution(9703080728592565039)
XLA Ops:
  0.0 0.0 copy-start
  0.0 0.0 copy-start.1
  0.0 2.3 %pack.1 = (bf16[7168,128]{1,0:T(8,128)(2,1)S(1)}, s32[8,128]{1,0:T(8,128)S(1)}) custom-call(s32[8,16]{1,0:T(8,128)} %bitcast.10, bf16[16,3584]{1,0:T(8,128)(2,1)} %tokens_ref.1), custom_call_target="tpu_custom_call" | custom-call | flops 20000000000 | bytes 1000 | tf_op jit(solution)/shard_map/pack/pallas_call | solution.py:72
  2.4 38.0 %all_to_all.10 = bf16[128,56,128]{2,1,0:T(8,128)(2,1)S(1)} all-to-all(bf16[128,56,128]{2,1,0:T(8,128)(2,1)S(1)} %bitcast.9), channel_id=1, replica_groups=mesh['node'=8,'local'=16] {'node','local'}, dimensions={0} | all-to-all | bytes 3670016 | tf_op jit(solution)/shard_map/all_to_all | solution.py:244
  40.4 0.0 copy-done
  40.4 0.0 copy-done.1
  40.4 6.7 %expert_ffn.1 = bf16[7168,128]{1,0:T(8,128)(2,1)S(1)} custom-call(bf16[7168,128]{1,0:T(8,128)(2,1)S(1)} %bitcast.6, bf16[1,3584,2048]{2,1,0:T(8,128)(2,1)S(1)} %copy-done, bf16[1,1024,3584]{2,1,0:T(8,128)(2,1)S(1)} %copy-done.1), custom_call_target="tpu_custom_call" | custom-call | flops 5637144576 | bytes 22020096 | tf_op jit(solution)/shard_map/expert_ffn/pallas_call | solution.py:150
  47.1 0.0 copy-start.2
  47.1 0.0 copy-start.3
  47.1 31.3 %all_to_all.11 = bf16[128,56,128]{2,1,0:T(8,128)(2,1)S(1)} all-to-all(bf16[128,56,128]{2,1,0:T(8,128)(2,1)S(1)} %bitcast.7), channel_id=1, replica_groups=mesh['node'=8,'local'=16] {'node','local'}, dimensions={0} | all-to-all | bytes 3670016 | tf_op jit(solution)/shard_map/all_to_all | solution.py:244
  78.4 0.0 copy-done.2
  78.4 0.0 copy-done.3
  78.4 1.9 %combine.1 = bf16[16,3584]{1,0:T(8,128)(2,1)} custom-call(s32[8,16]{1,0:T(8,128)S(1)} %bitcast.11, s32[8,128]{1,0:T(8,128)S(1)} %get-tuple-element.7.first_ref, bf16[8,16]{1,0:T(8,128)(2,1)S(1)} %bitcast.12, bf16[7168,128]{1,0:T(8,128)(2,1)S(1)} %bitcast.8), custom_call_target="tpu_custom_call" | custom-call | tf_op jit(solution)/shard_map/combine/pallas_call | solution.py:218
Async XLA Ops:
  0.0 40.4 %copy-start = (bf16[1,3584,2048]{2,1,0:T(8,128)(2,1)S(1)}, bf16[1,3584,2048]{2,1,0:T(8,128)(2,1)}, u32[]{:S(2)}) copy-start(bf16[1,3584,2048]{2,1,0:T(8,128)(2,1)} %gate_up_ref.1) | copy-start | bytes 44040196
  0.0 40.4 %copy-start.1 = (bf16[1,1024,3584]{2,1,0:T(8,128)(2,1)S(1)}, bf16[1,1024,3584]{2,1,0:T(8,128)(2,1)}, u32[]{:S(2)}) copy-start(bf16[1,1024,3584]{2,1,0:T(8,128)(2,1)} %down_ref.1) | copy-start | bytes 22020100
  47.1 31.4 %copy-start.2 = (s32[16,8]{0,1:T(8,128)S(1)}, s32[16,8]{0,1:T(8,128)}, u32[]{:S(2)}) copy-start(s32[16,8]{0,1:T(8,128)} %param.6) | copy-start | bytes 1540
  47.1 31.4 %copy-start.3 = (bf16[16,8]{0,1:T(8,128)(2,1)S(1)}, bf16[16,8]{0,1:T(8,128)(2,1)}, u32[]{:S(2)}) copy-start(bf16[16,8]{0,1:T(8,128)(2,1)} %param.7) | copy-start | bytes 772

commit v8 on v7

--- a/solution.py
+++ b/solution.py
@@ -147,13 +147,14 @@
     hidden = both // 2
     total = got.shape[0]
     slots = total * LANES // width
+    peers = slots // 2
     return pl.pallas_call(
         ffn_kernel,
         out_shape=jax.ShapeDtypeStruct(got.shape, BF16),
         in_specs=[pl.BlockSpec(memory_space=pltpu.VMEM)] * 3,
         out_specs=pl.BlockSpec(memory_space=pltpu.VMEM),
         scratch_shapes=[
-            pltpu.VMEM((total, LANES), F32),
+            pltpu.VMEM((total + total // peers, LANES), F32),
             pltpu.VMEM((slots, width), BF16),
             pltpu.VMEM((slots, hidden), BF16),
         ],
@@ -222,7 +223,7 @@
         out_specs=vmem,
         scratch_shapes=[
             pltpu.VMEM(got.shape, F32),
-            pltpu.VMEM((row_count * pitch, LANES), F32),
+            pltpu.VMEM(((row_count + 1) * pitch, LANES), F32),
             pltpu.VMEM(weight.shape, F32),
             pltpu.SMEM(route.shape, jnp.int32),
             pltpu.SMEM(first.shape, jnp.int32),

time: 80.4 us -> 80.5 us (level)
  no operation moved by 1% of the time
where the time goes in v8:
time: 80.5 us; the launch traced here: 80.3 us
  blocking collectives  69.4 us (86%)
  Pallas kernels  10.9 us (14%)
    all_to_all x2, blocking collectives, exchange(): lax.all_to_all(blocks, ('node', 'local'), split_axis=0, concat_axis=0, ti...  69.4 us
    pallas_call x1, Pallas kernels, expert_ffn(): pl.pallas_call(ffn_kernel, out_shape=jax.ShapeDtypeStruct(got.shape, BF16...  6.71 us
    pallas_call x1, Pallas kernels, pack(): pl.pallas_call(pack_kernel, out_shape=(jax.ShapeDtypeStruct((peers * pitc...  2.34 us
    pallas_call x1, Pallas kernels, combine(): pl.pallas_call(combine_kernel, out_shape=jax.ShapeDtypeStruct((row_count,...  1.87 us

profile of v8, /device:TPU:0, one launch (start us, length us, event | category | flops | bytes accessed | tf_op | source)
XLA Modules:
  0.0 80.3 jit_solution(5645967338259975266)
XLA Ops:
  0.0 0.0 copy-start
  0.0 0.0 copy-start.1
  0.0 2.3 %pack.1 = (bf16[7168,128]{1,0:T(8,128)(2,1)S(1)}, s32[8,128]{1,0:T(8,128)S(1)}) custom-call(s32[8,16]{1,0:T(8,128)} %bitcast.10, bf16[16,3584]{1,0:T(8,128)(2,1)} %tokens_ref.1), custom_call_target="tpu_custom_call" | custom-call | flops 20000000000 | bytes 1000 | tf_op jit(solution)/shard_map/pack/pallas_call | solution.py:72
  2.4 38.0 %all_to_all.10 = bf16[128,56,128]{2,1,0:T(8,128)(2,1)S(1)} all-to-all(bf16[128,56,128]{2,1,0:T(8,128)(2,1)S(1)} %bitcast.9), channel_id=1, replica_groups=mesh['node'=8,'local'=16] {'node','local'}, dimensions={0} | all-to-all | bytes 3670016 | tf_op jit(solution)/shard_map/all_to_all | solution.py:245
  40.4 0.0 copy-done
  40.4 0.0 copy-done.1
  40.4 6.7 %expert_ffn.1 = bf16[7168,128]{1,0:T(8,128)(2,1)S(1)} custom-call(bf16[7168,128]{1,0:T(8,128)(2,1)S(1)} %bitcast.6, bf16[1,3584,2048]{2,1,0:T(8,128)(2,1)S(1)} %copy-done, bf16[1,1024,3584]{2,1,0:T(8,128)(2,1)S(1)} %copy-done.1), custom_call_target="tpu_custom_call" | custom-call | flops 5637144576 | bytes 22020096 | tf_op jit(solution)/shard_map/expert_ffn/pallas_call | solution.py:151
  47.1 0.0 copy-start.2
  47.1 0.0 copy-start.3
  47.1 31.3 %all_to_all.11 = bf16[128,56,128]{2,1,0:T(8,128)(2,1)S(1)} all-to-all(bf16[128,56,128]{2,1,0:T(8,128)(2,1)S(1)} %bitcast.7), channel_id=1, replica_groups=mesh['node'=8,'local'=16] {'node','local'}, dimensions={0} | all-to-all | bytes 3670016 | tf_op jit(solution)/shard_map/all_to_all | solution.py:245
  78.5 0.0 copy-done.2
  78.5 0.0 copy-done.3
  78.5 1.9 %combine.1 = bf16[16,3584]{1,0:T(8,128)(2,1)} custom-call(s32[8,16]{1,0:T(8,128)S(1)} %bitcast.11, s32[8,128]{1,0:T(8,128)S(1)} %get-tuple-element.7.first_ref, bf16[8,16]{1,0:T(8,128)(2,1)S(1)} %bitcast.12, bf16[7168,128]{1,0:T(8,128)(2,1)S(1)} %bitcast.8), custom_call_target="tpu_custom_call" | custom-call | tf_op jit(solution)/shard_map/combine/pallas_call | solution.py:219
Async XLA Ops:
  0.0 40.4 %copy-start = (bf16[1,3584,2048]{2,1,0:T(8,128)(2,1)S(1)}, bf16[1,3584,2048]{2,1,0:T(8,128)(2,1)}, u32[]{:S(2)}) copy-start(bf16[1,3584,2048]{2,1,0:T(8,128)(2,1)} %gate_up_ref.1) | copy-start | bytes 44040196
  0.0 40.4 %copy-start.1 = (bf16[1,1024,3584]{2,1,0:T(8,128)(2,1)S(1)}, bf16[1,1024,3584]{2,1,0:T(8,128)(2,1)}, u32[]{:S(2)}) copy-start(bf16[1,1024,3584]{2,1,0:T(8,128)(2,1)} %down_ref.1) | copy-start | bytes 22020100
  47.1 31.4 %copy-start.2 = (s32[16,8]{0,1:T(8,128)S(1)}, s32[16,8]{0,1:T(8,128)}, u32[]{:S(2)}) copy-start(s32[16,8]{0,1:T(8,128)} %param.6) | copy-start | bytes 1540
  47.1 31.4 %copy-start.3 = (bf16[16,8]{0,1:T(8,128)(2,1)S(1)}, bf16[16,8]{0,1:T(8,128)(2,1)}, u32[]{:S(2)}) copy-start(bf16[16,8]{0,1:T(8,128)(2,1)} %param.7) | copy-start | bytes 772
